TPU v7x, 32 devices: a whole 2x2x4 slice. The times are simulated.
32 devices in a mesh: pipe: 2 (over core), dp: 4 (over y, x), rows: 4 (over z).
Axes of the slice: x: 2, y: 2, z: 4, core: 2. Of those that a mesh axis runs over, the one named last changes fastest.
Arguments:
- x_in: bfloat16 [4, 4, 8, 32, 512], P(None, 'dp', 'rows'), may hold values from -6 to 6
- pool_index: int32 [4, 4, 4, 16], P(None, 'dp', 'rows'), may hold values from 0 to 3
- task_mask: int32 [4, 4, 3], P(None, 'dp'), may hold values from 0 to 1, as said below
- task_cot: bfloat16 [3, 4, 4, 8, 32, 512], P(None, None, 'dp', 'rows'), may hold values from -8 to 8
- trunk_conv: bfloat16 [2, 2, 4608, 512], P('pipe', None, ('dp', 'rows')), may hold values from -0.09375 to 0.09375
- norm_gain: bfloat16 [2, 2, 512], P('pipe', None, ('dp', 'rows')), may hold values from 0.25 to 1.75
- norm_bias: bfloat16 [2, 2, 512], P('pipe', None, ('dp', 'rows')), may hold values from -3 to 3
- att_down: bfloat16 [2, 3, 512, 128], P('pipe', None, ('dp', 'rows')), may hold values from -0.25 to 0.25
- attention_up_weights: bfloat16 [2, 3, 128, 512], P('pipe', None, None, ('dp', 'rows')), may hold values from -1 to 1
- task_conv: bfloat16 [2, 3, 4608, 512], P('pipe', None, ('dp', 'rows')), may hold values from -0.09375 to 0.09375
Outputs:
- task_features: bfloat16 [2, 3, 4, 4, 8, 32, 512], P('pipe', None, None, 'dp', 'rows')
- input_grads: float32 [2, 4, 4, 8, 32, 512], P('pipe', None, 'dp', 'rows')
- trunk_grad: float32 [2, 2, 4608, 512], P('pipe', None, ('dp', 'rows'))
- gain_grad: float32 [2, 2, 512], P('pipe', None, ('dp', 'rows'))
- bias_grad: float32 [2, 2, 512], P('pipe', None, ('dp', 'rows'))
- down_grad: float32 [2, 3, 512, 128], P('pipe', None, ('dp', 'rows'))
- up_grad: float32 [2, 3, 128, 512], P('pipe', None, None, ('dp', 'rows'))
- task_grad: float32 [2, 3, 4608, 512], P('pipe', None, ('dp', 'rows'))
- nash_weights: float32 [3], replicated
Inputs may be any that keep to these rules, and one draw needn't show every extreme that they name: `task_mask`: each sample is labelled for one or two tasks.
All inputs are finite; a program needn't handle non-finite values.
Results may differ from a plain program's by a relative error of at most 0.018.
Values may be sent and summed in bfloat16 or wider, within the bound.
No kernel may reach another device: no remote copies, remote signals or barrier semaphores. Data moves between devices by JAX's collectives and lax.ppermute only.
A program may use at most 384 MiB of HBM per device.

v0:
```python
import jax
import jax.numpy as jnp
from jax import lax
from jax.sharding import PartitionSpec as P

NASH_ITERS = 3


eps = 1e-05


def extended_2(array, sides, width):
    for axis, dim in sides:
        peers, length = (lax.axis_size(axis), array.shape[dim])
        up = [(i, (i + 1) % peers) for i in range(peers - 1)]
        down = [(j, i) for i, j in up]
        last = lax.slice_in_dim(array, length - width, length, axis=dim)
        first = lax.slice_in_dim(array, 0, width, axis=dim)
        before = lax.ppermute(last, axis, up)
        after = lax.ppermute(first, axis, down)
        array = jnp.concatenate([before, array, after], axis=dim)
    return array


def from_behind(array, axis, by):
    peers = lax.axis_size(axis)
    pairs = [(i, i + by) for i in range(peers) if 0 <= i + by < peers]
    return lax.ppermute(array, axis, pairs)


def silu_slope(preact):
    sigmoid_val = jax.nn.sigmoid(preact)
    return sigmoid_val * (1.0 + preact * (1.0 - sigmoid_val))


def choose_side(condition, when_true, when_false):

    def either(true_leaf, false_leaf):
        return jnp.where(condition, true_leaf, false_leaf)

    return jax.tree.map(either, when_true, when_false)


def pool_cells(field, positions):
    leading = field.shape[:-4]
    samples, rows_n, cols_n, channels = field.shape[-4:]
    blocks = field.astype(jnp.float32).reshape(
        leading + (samples, rows_n // 2, 2, cols_n // 2, 2, channels)
    )
    blocks = jnp.moveaxis(blocks, -4, -3).reshape(
        leading + (samples, rows_n // 2, cols_n // 2, 4, channels)
    )
    return jnp.sum(blocks * positions[..., None], axis=-2)


def unpool_cells(small, positions):
    leading = small.shape[:-4]
    samples, rows_h, cols_h, channels = small.shape[-4:]
    blocks = small.astype(jnp.float32)[..., None, :] * positions[..., None]
    blocks = blocks.reshape(leading + (samples, rows_h, cols_h, 2, 2, channels))
    blocks = jnp.moveaxis(blocks, -3, -4)
    return blocks.reshape(leading + (samples, 2 * rows_h, 2 * cols_h, channels))


def gather_taps(padded, rows_n, cols_n):
    stencil = [
        padded[:, :, offset // 3 : offset // 3 + rows_n, offset % 3 : offset % 3 + cols_n, :]
        for offset in range(9)
    ]
    return jnp.concatenate(stencil, axis=-1)


def conv_forward(field, weight):
    extended = extended_2(field, (("rows", 2),), 1)
    padded = jnp.pad(extended, ((0, 0), (0, 0), (0, 0), (1, 1), (0, 0)))
    stencil = gather_taps(padded, field.shape[2], field.shape[3])
    conv_out = jnp.einsum("ksrwq,kqd->ksrwd", stencil, weight, preferred_element_type=jnp.float32)
    return (conv_out, padded)


def conv_backward(padded, grad_out, weight, wanted):
    rows_n, cols_n = (grad_out.shape[2], grad_out.shape[3])
    extended = extended_2(grad_out, (("rows", 2),), 1)
    beside_all = jnp.pad(extended, ((0, 0), (0, 0), (0, 0), (1, 1), (0, 0)))
    flipped = jnp.stack(
        [
            beside_all[
                :,
                :,
                2 - offset // 3 : 2 - offset // 3 + rows_n,
                2 - offset % 3 : 2 - offset % 3 + cols_n,
                :,
            ]
            for offset in range(9)
        ],
        axis=-2,
    )
    kernel = weight.reshape(weight.shape[0], 9, weight.shape[2], weight.shape[2])
    grad_in = jnp.einsum("ksrwtd,ktcd->ksrwc", flipped, kernel, preferred_element_type=jnp.float32)
    weight_grad = None
    if wanted:
        weight_grad = jnp.einsum(
            "ksrwq,ksrwd->kqd",
            gather_taps(padded, rows_n, cols_n),
            grad_out,
            preferred_element_type=jnp.float32,
        )
    return (grad_in, weight_grad)


def norm_moments(conv_out, pixel_count):
    center = lax.psum(jnp.sum(conv_out, axis=(0, 1, 2, 3)), ("dp", "rows")) / pixel_count
    spread = (
        lax.psum(jnp.sum(jnp.square(conv_out - center), axis=(0, 1, 2, 3)), ("dp", "rows"))
        / pixel_count
    )
    return (center, lax.rsqrt(spread + eps))


def section_forward(section_input, carried, positions, params, stats, pixel_count):
    trunk_maps, gain_rows, bias_rows, down_maps, upward_maps, task_maps = params
    hidden = section_input[None]
    layers = []
    moments = []
    for section_layer in range(2):
        conv_out, padded = conv_forward(hidden, trunk_maps[section_layer][None])
        if stats is None:
            center, inverse_std = norm_moments(conv_out, pixel_count)
        else:
            center, inverse_std = stats[section_layer]
        normed = (conv_out - center) * inverse_std
        preact = gain_rows[section_layer] * normed + bias_rows[section_layer]
        layers.append((padded, normed, preact))
        moments.append((center, inverse_std))
        hidden = jax.nn.silu(preact).astype(jnp.bfloat16)
    mixture = (hidden.astype(jnp.float32) + carried.astype(jnp.float32)).astype(jnp.bfloat16)
    inner_act = jnp.einsum(
        "tsrwc,tca->tsrwa", mixture, down_maps, preferred_element_type=jnp.float32
    )
    active_mask_flag = jax.nn.silu(inner_act).astype(jnp.bfloat16)
    class_logits = jnp.einsum(
        "zfhpv,zvm->zfhpm", active_mask_flag, upward_maps, preferred_element_type=jnp.float32
    )
    gating = jax.nn.sigmoid(class_logits)
    product = (gating * hidden.astype(jnp.float32)).astype(jnp.bfloat16)
    features, padded_task = conv_forward(product, task_maps)
    return {
        "layers": layers,
        "moments": moments,
        "shared": hidden,
        "mixture": mixture,
        "inner_act": inner_act,
        "active": active_mask_flag,
        "gating": gating,
        "padded_task": padded_task,
        "features": features,
        "section_input": section_input,
        "carried": carried,
        "positions": positions,
    }


def heads_backward(saved_record, grad_feats, params, wanted):
    down_maps, upward_maps, task_maps = (params[3], params[4], params[5])
    task_back, task_slope = conv_backward(
        saved_record["padded_task"], grad_feats, task_maps, wanted
    )
    shared = saved_record["shared"].astype(jnp.float32)
    gating = saved_record["gating"]
    logits_gradient = (task_back * shared * gating * (1.0 - gating)).astype(jnp.bfloat16)
    grad_active = jnp.einsum(
        "qubef,qxf->qubex", logits_gradient, upward_maps, preferred_element_type=jnp.float32
    )
    grad_inner = (grad_active * silu_slope(saved_record["inner_act"])).astype(jnp.bfloat16)
    grad_mixture = jnp.einsum(
        "tsrwa,tca->tsrwc", grad_inner, down_maps, preferred_element_type=jnp.float32
    )
    through = task_back * gating + grad_mixture
    slopes = None
    if wanted:
        slope_up = jnp.einsum(
            "munfg,munfq->mgq",
            saved_record["active"],
            logits_gradient,
            preferred_element_type=jnp.float32,
        )
        slope_down = jnp.einsum(
            "tsrwc,tsrwa->tca",
            saved_record["mixture"],
            grad_inner,
            preferred_element_type=jnp.float32,
        )
        slopes = (slope_down, slope_up, task_slope)
    return (through, grad_mixture, slopes)


def trunk_backward(saved_record, grad_shared, params, pixel_count):
    trunk_maps, gain_rows = (params[0], params[1])
    grad_hidden = grad_shared
    conv_grads = [None, None]
    gain_grads = [None, None]
    bias_grads = [None, None]
    for section_layer in (1, 0):
        padded, normed, preact = saved_record["layers"][section_layer]
        inverse_std = saved_record["moments"][section_layer][1]
        grad_pre = grad_hidden * silu_slope(preact)
        bias_part = jnp.sum(grad_pre, axis=(0, 1, 2, 3))
        gain_part = jnp.sum(grad_pre * normed, axis=(0, 1, 2, 3))
        bias_total, gain_total = lax.psum((bias_part, gain_part), ("dp", "rows"))
        grad_conv = (
            inverse_std
            * gain_rows[section_layer]
            * (grad_pre - bias_total / pixel_count - normed * gain_total / pixel_count)
        )
        grad_hidden, weight_grad = conv_backward(
            padded, grad_conv.astype(jnp.bfloat16), trunk_maps[section_layer][None], True
        )
        conv_grads[section_layer] = weight_grad[0]
        gain_grads[section_layer] = gain_part
        bias_grads[section_layer] = bias_part
    return (grad_hidden, jnp.stack(conv_grads), jnp.stack(gain_grads), jnp.stack(bias_grads))


def solve_small(matrix, right_side):
    cofactor = [
        [
            matrix[1, 1] * matrix[2, 2] - matrix[1, 2] * matrix[2, 1],
            matrix[1, 2] * matrix[2, 0] - matrix[1, 0] * matrix[2, 2],
            matrix[1, 0] * matrix[2, 1] - matrix[1, 1] * matrix[2, 0],
        ],
        [
            matrix[0, 2] * matrix[2, 1] - matrix[0, 1] * matrix[2, 2],
            matrix[0, 0] * matrix[2, 2] - matrix[0, 2] * matrix[2, 0],
            matrix[0, 1] * matrix[2, 0] - matrix[0, 0] * matrix[2, 1],
        ],
        [
            matrix[0, 1] * matrix[1, 2] - matrix[0, 2] * matrix[1, 1],
            matrix[0, 2] * matrix[1, 0] - matrix[0, 0] * matrix[1, 2],
            matrix[0, 0] * matrix[1, 1] - matrix[0, 1] * matrix[1, 0],
        ],
    ]
    determinant = (
        matrix[0, 0] * cofactor[0][0]
        + matrix[0, 1] * cofactor[0][1]
        + matrix[0, 2] * cofactor[0][2]
    )
    answer = [
        (
            cofactor[0][col_index] * right_side[0]
            + cofactor[1][col_index] * right_side[1]
            + cofactor[2][col_index] * right_side[2]
        )
        / determinant
        for col_index in range(3)
    ]
    return jnp.stack(answer)


def nash_solve(gram_sum):
    trace_mean = (gram_sum[0, 0] + gram_sum[1, 1] + gram_sum[2, 2]) / 3.0 + 1e-06
    normalized = gram_sum / trace_mean
    diagonal = jnp.stack([normalized[0, 0], normalized[1, 1], normalized[2, 2]])
    nash_alpha = lax.rsqrt(diagonal + 1e-06)
    for sweep_index in range(NASH_ITERS):
        residual = jnp.sum(normalized * nash_alpha[None, :], axis=1) - 1.0 / nash_alpha
        curvature = normalized + jnp.diag(1.0 / (nash_alpha * nash_alpha))
        update = solve_small(curvature, residual)
        nash_alpha = nash_alpha * jnp.exp(-0.5 * jnp.tanh(update / nash_alpha))
    return nash_alpha


def on_device(
    x_in,
    pool_index,
    task_mask,
    task_cot,
    trunk_conv,
    norm_gain,
    norm_bias,
    att_down,
    attention_up_weights,
    task_conv,
):
    micro_count = x_in.shape[0]
    tasks_n = task_cot.shape[0]
    decoder_side = lax.axis_index("pipe") == 1
    pixel_count = (
        x_in.shape[1] * x_in.shape[2] * x_in.shape[3] * lax.axis_size("dp") * lax.axis_size("rows")
    )
    pieces = (
        lax.all_gather(trunk_conv, ("dp", "rows"), axis=2, tiled=True),
        lax.all_gather(norm_gain, ("dp", "rows"), axis=2, tiled=True),
        lax.all_gather(norm_bias, ("dp", "rows"), axis=2, tiled=True),
        lax.all_gather(att_down, ("dp", "rows"), axis=2, tiled=True),
        lax.all_gather(attention_up_weights, ("dp", "rows"), axis=3, tiled=True),
        lax.all_gather(task_conv, ("dp", "rows"), axis=2, tiled=True),
    )
    params = (
        pieces[0][0],
        pieces[1][0].astype(jnp.float32),
        pieces[2][0].astype(jnp.float32),
        pieces[3][0],
        pieces[4][0],
        pieces[5][0],
    )
    onehot = (pool_index[..., None] == jnp.arange(4, dtype=jnp.int32)).astype(jnp.float32)
    mask_weights = jnp.transpose(task_mask, (0, 2, 1)).astype(jnp.float32)
    no_carry = jnp.zeros((tasks_n,) + x_in.shape[1:], jnp.bfloat16)
    incoming = jnp.zeros(
        (tasks_n + 1, x_in.shape[1], x_in.shape[2] // 2, x_in.shape[3] // 2, x_in.shape[4]),
        jnp.bfloat16,
    )
    records = []
    for period in range(micro_count + 1):
        enc_index = min(period, micro_count - 1)
        dec_index = max(period - 1, 0)
        positions = jnp.where(decoder_side, onehot[dec_index], onehot[enc_index])
        section_input = jnp.where(
            decoder_side, unpool_cells(incoming[0], positions).astype(jnp.bfloat16), x_in[enc_index]
        )
        carried = jnp.where(
            decoder_side, unpool_cells(incoming[1:], positions).astype(jnp.bfloat16), no_carry
        )
        saved_record = section_forward(section_input, carried, positions, params, None, pixel_count)
        records.append(saved_record)
        if period < micro_count:
            outgoing = jnp.concatenate(
                [
                    pool_cells(saved_record["shared"], positions),
                    pool_cells(saved_record["features"].astype(jnp.bfloat16), positions),
                ],
                axis=0,
            )
            incoming = from_behind(outgoing.astype(jnp.bfloat16), "pipe", 1)
    kept_records = []
    gram_sum = jnp.zeros((tasks_n, tasks_n), jnp.float32)
    for micro_index in range(micro_count):
        source_input = choose_side(decoder_side, records[micro_index + 1], records[micro_index])
        chosen = section_forward(
            source_input["section_input"],
            source_input["carried"],
            source_input["positions"],
            params,
            source_input["moments"],
            pixel_count,
        )
        kept_records.append(chosen)
        plain_cot = task_cot[:, micro_index] * mask_weights[micro_index][:, :, None, None, None]
        through, unused_mixture, unused_slopes = heads_backward(
            chosen, plain_cot.astype(jnp.bfloat16), params, False
        )
        flattened = through.reshape(tasks_n, -1)
        partial_gram = jnp.dot(flattened, flattened.T, precision=lax.Precision.HIGHEST)
        gram_sum = gram_sum + jnp.where(decoder_side, partial_gram, 0.0)
    gram_sum = lax.psum(gram_sum, ("pipe", "dp", "rows"))
    nash_alpha = nash_solve(gram_sum)
    returning = jnp.zeros_like(incoming)
    start_grads = []
    trunk_sum, gain_sum, bias_sum = (0.0, 0.0, 0.0)
    down_sum, up_sum, task_sum = (0.0, 0.0, 0.0)
    for period in range(micro_count + 1):
        dec_index = max(micro_count - 1 - period, 0)
        enc_index = min(micro_count - period, micro_count - 1)
        active_flag = 1.0 if period < micro_count else 0.0
        chosen = choose_side(decoder_side, kept_records[dec_index], kept_records[enc_index])
        positions = chosen["positions"]
        weighted = (
            nash_alpha[:, None, None, None, None]
            * mask_weights[dec_index][:, :, None, None, None]
            * task_cot[:, dec_index].astype(jnp.float32)
            * active_flag
        )
        grad_feats = jnp.where(
            decoder_side, weighted, unpool_cells(returning[1:], positions)
        ).astype(jnp.bfloat16)
        through, grad_mixture, slopes = heads_backward(chosen, grad_feats, params, True)
        down_sum = down_sum + slopes[0]
        up_sum = up_sum + slopes[1]
        task_sum = task_sum + slopes[2]
        pooled_back = jnp.where(decoder_side, 0.0, unpool_cells(returning[0:1], positions))
        grad_shared = jnp.sum(through, axis=0, keepdims=True) + pooled_back
        grad_start, conv_grads, gain_grads, bias_grads = trunk_backward(
            chosen, grad_shared, params, pixel_count
        )
        start_grads.append(grad_start[0])
        trunk_sum = trunk_sum + conv_grads
        gain_sum = gain_sum + gain_grads
        bias_sum = bias_sum + bias_grads
        if period < micro_count:
            outgoing = jnp.concatenate(
                [pool_cells(grad_start, positions), pool_cells(grad_mixture, positions)], axis=0
            )
            returning = from_behind(outgoing.astype(jnp.bfloat16), "pipe", -1)
    features_out = jnp.stack(
        [
            jnp.where(
                decoder_side, records[micro_index + 1]["features"], records[micro_index]["features"]
            )
            for micro_index in range(micro_count)
        ],
        axis=1,
    ).astype(jnp.bfloat16)
    grads_out = jnp.stack(
        [
            jnp.where(
                decoder_side,
                start_grads[micro_count - 1 - micro_index],
                start_grads[micro_count - micro_index],
            )
            for micro_index in range(micro_count)
        ],
        axis=0,
    )
    shares = (
        lax.psum_scatter(trunk_sum[None], ("dp", "rows"), scatter_dimension=2, tiled=True),
        lax.psum_scatter(gain_sum[None], ("dp", "rows"), scatter_dimension=2, tiled=True),
        lax.psum_scatter(bias_sum[None], ("dp", "rows"), scatter_dimension=2, tiled=True),
        lax.psum_scatter(down_sum[None], ("dp", "rows"), scatter_dimension=2, tiled=True),
        lax.psum_scatter(up_sum[None], ("dp", "rows"), scatter_dimension=3, tiled=True),
        lax.psum_scatter(task_sum[None], ("dp", "rows"), scatter_dimension=2, tiled=True),
    )
    return (
        features_out[None],
        grads_out[None],
        shares[0],
        shares[1],
        shares[2],
        shares[3],
        shares[4],
        shares[5],
        nash_alpha,
    )


def solution(mesh):
    in_specs = (
        P(None, "dp", "rows", None, None),
        P(None, "dp", "rows", None),
        P(None, "dp", None),
        P(None, None, "dp", "rows", None, None),
        P("pipe", None, ("dp", "rows"), None),
        P("pipe", None, ("dp", "rows")),
        P("pipe", None, ("dp", "rows")),
        P("pipe", None, ("dp", "rows"), None),
        P("pipe", None, None, ("dp", "rows")),
        P("pipe", None, ("dp", "rows"), None),
    )
    out_specs = (
        P("pipe", None, None, "dp", "rows", None, None),
        P("pipe", None, "dp", "rows", None, None),
        P("pipe", None, ("dp", "rows"), None),
        P("pipe", None, ("dp", "rows")),
        P("pipe", None, ("dp", "rows")),
        P("pipe", None, ("dp", "rows"), None),
        P("pipe", None, None, ("dp", "rows")),
        P("pipe", None, ("dp", "rows"), None),
        P(),
    )
    return jax.shard_map(
        on_device, mesh=mesh, in_specs=in_specs, out_specs=out_specs, check_vma=False
    )
```

profile of v0, /device:TPU:0, one launch (start us, length us, event | category | flops | bytes accessed | tf_op | source)
XLA Modules:
  0.0 3183.4 jit_solution(9839423032521395061)
XLA Ops:
  27.3 47.6 %all_gather.20 = bf16[1,2,512]{1,0,2:T(2,128)(2,1)S(1)} all-gather(bf16[1,2,32]{1,0,2:T(2,128)(2,1)S(1)} %copy.230), channel_id=1, replica_groups=mesh['pipe'=2,'dp'=4,'rows'=4] {'dp','rows'}, dimensions={2}, use_global_device_ids=true | all-gather | bytes 2176 | tf_op jit(solution)/shard_map/all_gather | solution.py:293
  75.2 42.1 %all_gather.18 = bf16[1,2,512]{1,0,2:T(2,128)(2,1)S(1)} all-gather(bf16[1,2,32]{1,0,2:T(2,128)(2,1)S(1)} %copy.228), channel_id=1, replica_groups=mesh['pipe'=2,'dp'=4,'rows'=4] {'dp','rows'}, dimensions={2}, use_global_device_ids=true | all-gather | bytes 2176 | tf_op jit(solution)/shard_map/all_gather | solution.py:292
  122.9 42.2 %all_gather.22 = bf16[1,3,128,512]{2,3,1,0:T(8,128)(2,1)S(1)} all-gather(bf16[1,3,128,32]{2,3,1,0:T(8,128)(2,1)S(1)} %copy-done.167), channel_id=1, replica_groups=mesh['pipe'=2,'dp'=4,'rows'=4] {'dp','rows'}, dimensions={3}, use_global_device_ids=true | all-gather | bytes 417792 | tf_op jit(solution)/shard_map/all_gather | solution.py:295
  165.1 46.2 %all_gather.21 = bf16[1,3,512,128]{3,2,1,0:T(8,128)(2,1)S(1)} all-gather(bf16[1,3,32,128]{3,2,1,0:T(8,128)(2,1)S(1)} %copy-done.168), channel_id=1, replica_groups=mesh['pipe'=2,'dp'=4,'rows'=4] {'dp','rows'}, dimensions={2}, use_global_device_ids=true | all-gather | bytes 417792 | tf_op jit(solution)/shard_map/all_gather | solution.py:294
  259.5 40.4 %psum.287 = f32[512]{0:T(512)S(1)} all-reduce(f32[512]{0:T(512)S(1)} %get-tuple-element.371), channel_id=1, replica_groups=mesh['pipe'=2,'dp'=4,'rows'=4] {'dp','rows'}, use_global_device_ids=true, to_apply=%region_1.2 | all-reduce | flops 512 | bytes 4096 | tf_op jit(solution)/shard_map/psum | solution.py:112
  300.0 37.7 %psum.288 = f32[512]{0:T(512)S(1)} all-reduce(f32[512]{0:T(512)S(1)} %multiply_reduce_fusion.19), channel_id=1, replica_groups=mesh['pipe'=2,'dp'=4,'rows'=4] {'dp','rows'}, use_global_device_ids=true, to_apply=%region_3.4 | all-reduce | flops 512 | bytes 4096 | tf_op jit(solution)/shard_map/psum | solution.py:114
  343.9 7.9 fusion.712
  355.4 38.6 %psum.289 = f32[512]{0:T(512)S(1)} all-reduce(f32[512]{0:T(512)S(1)} %get-tuple-element.373), channel_id=1, replica_groups=mesh['pipe'=2,'dp'=4,'rows'=4] {'dp','rows'}, use_global_device_ids=true, to_apply=%region_5.6 | all-reduce | flops 512 | bytes 4096 | tf_op jit(solution)/shard_map/psum | solution.py:112
  394.0 36.9 %psum.290 = f32[512]{0:T(512)S(1)} all-reduce(f32[512]{0:T(512)S(1)} %multiply_reduce_fusion.18), channel_id=1, replica_groups=mesh['pipe'=2,'dp'=4,'rows'=4] {'dp','rows'}, use_global_device_ids=true, to_apply=%region_7.8 | all-reduce | flops 512 | bytes 4096 | tf_op jit(solution)/shard_map/psum | solution.py:114
  440.1 7.5 fusion.12
  449.6 10.8 fusion.74
  460.5 8.4 fusion.76
  468.8 8.3 fusion.78
  477.1 10.7 fusion.80
  499.4 40.1 %psum.291 = f32[512]{0:T(512)S(1)} all-reduce(f32[512]{0:T(512)S(1)} %get-tuple-element.375), channel_id=1, replica_groups=mesh['pipe'=2,'dp'=4,'rows'=4] {'dp','rows'}, use_global_device_ids=true, to_apply=%region_11.12 | all-reduce | flops 512 | bytes 4096 | tf_op jit(solution)/shard_map/psum | solution.py:112
  540.1 36.7 %psum.292 = f32[512]{0:T(512)S(1)} all-reduce(f32[512]{0:T(512)S(1)} %multiply_reduce_fusion.17), channel_id=1, replica_groups=mesh['pipe'=2,'dp'=4,'rows'=4] {'dp','rows'}, use_global_device_ids=true, to_apply=%region_13.14 | all-reduce | flops 512 | bytes 4096 | tf_op jit(solution)/shard_map/psum | solution.py:114
  588.4 39.2 %psum.293 = f32[512]{0:T(512)S(1)} all-reduce(f32[512]{0:T(512)S(1)} %get-tuple-element.377), channel_id=1, replica_groups=mesh['pipe'=2,'dp'=4,'rows'=4] {'dp','rows'}, use_global_device_ids=true, to_apply=%region_15.16 | all-reduce | flops 512 | bytes 4096 | tf_op jit(solution)/shard_map/psum | solution.py:112
  627.7 36.7 %psum.294 = f32[512]{0:T(512)S(1)} all-reduce(f32[512]{0:T(512)S(1)} %multiply_reduce_fusion.16), channel_id=1, replica_groups=mesh['pipe'=2,'dp'=4,'rows'=4] {'dp','rows'}, use_global_device_ids=true, to_apply=%region_17.18 | all-reduce | flops 512 | bytes 4096 | tf_op jit(solution)/shard_map/psum | solution.py:114
  674.2 7.5 fusion.10
  701.8 39.1 %psum.295 = f32[512]{0:T(512)S(1)} all-reduce(f32[512]{0:T(512)S(1)} %get-tuple-element.379), channel_id=1, replica_groups=mesh['pipe'=2,'dp'=4,'rows'=4] {'dp','rows'}, use_global_device_ids=true, to_apply=%region_21.22 | all-reduce | flops 512 | bytes 4096 | tf_op jit(solution)/shard_map/psum | solution.py:112
  740.9 36.7 %psum.296 = f32[512]{0:T(512)S(1)} all-reduce(f32[512]{0:T(512)S(1)} %multiply_reduce_fusion.15), channel_id=1, replica_groups=mesh['pipe'=2,'dp'=4,'rows'=4] {'dp','rows'}, use_global_device_ids=true, to_apply=%region_23.24 | all-reduce | flops 512 | bytes 4096 | tf_op jit(solution)/shard_map/psum | solution.py:114
  789.4 39.2 %psum.297 = f32[512]{0:T(512)S(1)} all-reduce(f32[512]{0:T(512)S(1)} %get-tuple-element.381), channel_id=1, replica_groups=mesh['pipe'=2,'dp'=4,'rows'=4] {'dp','rows'}, use_global_device_ids=true, to_apply=%region_25.26 | all-reduce | flops 512 | bytes 4096 | tf_op jit(solution)/shard_map/psum | solution.py:112
  828.7 36.7 %psum.298 = f32[512]{0:T(512)S(1)} all-reduce(f32[512]{0:T(512)S(1)} %multiply_reduce_fusion.14), channel_id=1, replica_groups=mesh['pipe'=2,'dp'=4,'rows'=4] {'dp','rows'}, use_global_device_ids=true, to_apply=%region_27.28 | all-reduce | flops 512 | bytes 4096 | tf_op jit(solution)/shard_map/psum | solution.py:114
  875.2 7.5 fusion.8
  907.5 39.4 %psum.299 = f32[512]{0:T(512)S(1)} all-reduce(f32[512]{0:T(512)S(1)} %get-tuple-element.383), channel_id=1, replica_groups=mesh['pipe'=2,'dp'=4,'rows'=4] {'dp','rows'}, use_global_device_ids=true, to_apply=%region_31.32 | all-reduce | flops 512 | bytes 4096 | tf_op jit(solution)/shard_map/psum | solution.py:112
  947.0 36.8 %psum.300 = f32[512]{0:T(512)S(1)} all-reduce(f32[512]{0:T(512)S(1)} %multiply_reduce_fusion.13), channel_id=1, replica_groups=mesh['pipe'=2,'dp'=4,'rows'=4] {'dp','rows'}, use_global_device_ids=true, to_apply=%region_33.34 | all-reduce | flops 512 | bytes 4096 | tf_op jit(solution)/shard_map/psum | solution.py:114
  1007.1 36.8 %psum.301 = f32[512]{0:T(512)S(1)} all-reduce(f32[512]{0:T(512)S(1)} %get-tuple-element.385), channel_id=1, replica_groups=mesh['pipe'=2,'dp'=4,'rows'=4] {'dp','rows'}, use_global_device_ids=true, to_apply=%region_35.36 | all-reduce | flops 512 | bytes 4096 | tf_op jit(solution)/shard_map/psum | solution.py:112
  1043.9 38.8 %psum.302 = f32[512]{0:T(512)S(1)} all-reduce(f32[512]{0:T(512)S(1)} %multiply_reduce_fusion.12), channel_id=1, replica_groups=mesh['pipe'=2,'dp'=4,'rows'=4] {'dp','rows'}, use_global_device_ids=true, to_apply=%region_37.38 | all-reduce | flops 512 | bytes 4096 | tf_op jit(solution)/shard_map/psum | solution.py:114
  1092.4 7.5 fusion.6
  1122.8 38.7 %psum.303 = f32[512]{0:T(512)S(1)} all-reduce(f32[512]{0:T(512)S(1)} %get-tuple-element.387), channel_id=1, replica_groups=mesh['pipe'=2,'dp'=4,'rows'=4] {'dp','rows'}, use_global_device_ids=true, to_apply=%region_41.42 | all-reduce | flops 512 | bytes 4096 | tf_op jit(solution)/shard_map/psum | solution.py:112
  1161.6 36.8 %psum.304 = f32[512]{0:T(512)S(1)} all-reduce(f32[512]{0:T(512)S(1)} %multiply_reduce_fusion.11), channel_id=1, replica_groups=mesh['pipe'=2,'dp'=4,'rows'=4] {'dp','rows'}, use_global_device_ids=true, to_apply=%region_43.44 | all-reduce | flops 512 | bytes 4096 | tf_op jit(solution)/shard_map/psum | solution.py:114
  1241.4 38.7 %psum.305 = f32[512]{0:T(512)S(1)} all-reduce(f32[512]{0:T(512)S(1)} %get-tuple-element.391), channel_id=1, replica_groups=mesh['pipe'=2,'dp'=4,'rows'=4] {'dp','rows'}, use_global_device_ids=true, to_apply=%region_45.46 | all-reduce | flops 512 | bytes 4096 | tf_op jit(solution)/shard_map/psum | solution.py:112
  1280.2 36.7 %psum.306 = f32[512]{0:T(512)S(1)} all-reduce(f32[512]{0:T(512)S(1)} %multiply_reduce_fusion.10), channel_id=1, replica_groups=mesh['pipe'=2,'dp'=4,'rows'=4] {'dp','rows'}, use_global_device_ids=true, to_apply=%region_47.48 | all-reduce | flops 512 | bytes 4096 | tf_op jit(solution)/shard_map/psum | solution.py:114
  1352.8 40.9 %psum.307 = f32[3,3]{1,0:T(4,128)S(1)} all-reduce(f32[3,3]{1,0:T(4,128)S(1)} %fusion.217), channel_id=1, replica_groups=mesh['pipe'=2,'dp'=4,'rows'=4] {'pipe','dp','rows'}, use_global_device_ids=true, to_apply=%region_48.49 | all-reduce | flops 9 | bytes 72 | tf_op jit(solution)/shard_map/psum | solution.py:355
  1506.8 7.6 fusion.72
  1516.6 42.5 %all-reduce.56 = (f32[512]{0:T(512)}, f32[512]{0:T(512)S(1)}) all-reduce(f32[512]{0:T(512)S(1)} %get-tuple-element.68, f32[512]{0:T(512)S(1)} %get-tuple-element.67), channel_id=1, replica_groups=mesh['pipe'=2,'dp'=4,'rows'=4] {'dp','rows'}, use_global_device_ids=true, to_apply=%region_56.57 | all-reduce | flops 1024 | bytes 8192 | tf_op jit(solution)/shard_map/psum | solution.py:209
  1567.2 6.1 convolution_bitcast_fusion.8
  1582.3 37.3 %all-reduce.55 = (f32[512]{0:T(512)}, f32[512]{0:T(512)S(1)}) all-reduce(f32[512]{0:T(512)S(1)} %get-tuple-element.66, f32[512]{0:T(512)S(1)} %get-tuple-element.65), channel_id=1, replica_groups=mesh['pipe'=2,'dp'=4,'rows'=4] {'dp','rows'}, use_global_device_ids=true, to_apply=%region_60.61 | all-reduce | flops 1024 | bytes 8192 | tf_op jit(solution)/shard_map/psum | solution.py:209
  1636.6 6.1 convolution_bitcast_fusion.9
  1662.3 7.6 fusion.70
  1676.5 38.1 %all-reduce.54 = (f32[512]{0:T(512)S(1)}, f32[512]{0:T(512)S(1)}) all-reduce(f32[512]{0:T(512)S(1)} %get-tuple-element.64, f32[512]{0:T(512)S(1)} %get-tuple-element.63), channel_id=1, replica_groups=mesh['pipe'=2,'dp'=4,'rows'=4] {'dp','rows'}, use_global_device_ids=true, to_apply=%region_67.68 | all-reduce | flops 1024 | bytes 8192 | tf_op jit(solution)/shard_map/psum | solution.py:209
  1720.8 6.1 convolution_bitcast_fusion.6
  1730.4 37.9 %all-reduce.53 = (f32[512]{0:T(512)}, f32[512]{0:T(512)S(1)}) all-reduce(f32[512]{0:T(512)S(1)} %get-tuple-element.62, f32[512]{0:T(512)S(1)} %get-tuple-element.61), channel_id=1, replica_groups=mesh['pipe'=2,'dp'=4,'rows'=4] {'dp','rows'}, use_global_device_ids=true, to_apply=%region_71.72 | all-reduce | flops 1024 | bytes 8192 | tf_op jit(solution)/shard_map/psum | solution.py:209
  1806.0 7.6 fusion.68
  1820.9 38.5 %all-reduce.52 = (f32[512]{0:T(512)S(1)}, f32[512]{0:T(512)S(1)}) all-reduce(f32[512]{0:T(512)S(1)} %get-tuple-element.60, f32[512]{0:T(512)S(1)} %get-tuple-element.59), channel_id=1, replica_groups=mesh['pipe'=2,'dp'=4,'rows'=4] {'dp','rows'}, use_global_device_ids=true, to_apply=%region_78.79 | all-reduce | flops 1024 | bytes 8192 | tf_op jit(solution)/shard_map/psum | solution.py:209
  1874.2 38.0 %all-reduce.51 = (f32[512]{0:T(512)}, f32[512]{0:T(512)S(1)}) all-reduce(f32[512]{0:T(512)S(1)} %get-tuple-element.58, f32[512]{0:T(512)S(1)} %get-tuple-element.57), channel_id=1, replica_groups=mesh['pipe'=2,'dp'=4,'rows'=4] {'dp','rows'}, use_global_device_ids=true, to_apply=%region_82.83 | all-reduce | flops 1024 | bytes 8192 | tf_op jit(solution)/shard_map/psum | solution.py:209
  1926.1 6.1 convolution_bitcast_fusion.5
  1946.6 7.6 fusion.66
  1955.8 39.2 %all-reduce.50 = (f32[512]{0:T(512)S(1)}, f32[512]{0:T(512)S(1)}) all-reduce(f32[512]{0:T(512)S(1)} %get-tuple-element.56, f32[512]{0:T(512)S(1)} %get-tuple-element.55), channel_id=1, replica_groups=mesh['pipe'=2,'dp'=4,'rows'=4] {'dp','rows'}, use_global_device_ids=true, to_apply=%region_89.90 | all-reduce | flops 1024 | bytes 8192 | tf_op jit(solution)/shard_map/psum | solution.py:209
  2013.7 36.8 %all-reduce.49 = (f32[512]{0:T(512)S(1)}, f32[512]{0:T(512)S(1)}) all-reduce(f32[512]{0:T(512)S(1)} %get-tuple-element.54, f32[512]{0:T(512)S(1)} %get-tuple-element.53), channel_id=1, replica_groups=mesh['pipe'=2,'dp'=4,'rows'=4] {'dp','rows'}, use_global_device_ids=true, to_apply=%region_93.94 | all-reduce | flops 1024 | bytes 8192 | tf_op jit(solution)/shard_map/psum | solution.py:209
  2079.3 7.6 fusion.64
  2088.7 39.1 %all-reduce.48 = (f32[512]{0:T(512)S(1)}, f32[512]{0:T(512)S(1)}) all-reduce(f32[512]{0:T(512)S(1)} %get-tuple-element.52, f32[512]{0:T(512)S(1)} %get-tuple-element.51), channel_id=1, replica_groups=mesh['pipe'=2,'dp'=4,'rows'=4] {'dp','rows'}, use_global_device_ids=true, to_apply=%region_100.101 | all-reduce | flops 1024 | bytes 8192 | tf_op jit(solution)/shard_map/psum | solution.py:209
  2160.4 38.8 %all-reduce.47 = (f32[512]{0:T(512)S(1)}, f32[512]{0:T(512)S(1)}) all-reduce(f32[512]{0:T(512)S(1)} %get-tuple-element.50, f32[512]{0:T(512)S(1)} %get-tuple-element.49), channel_id=1, replica_groups=mesh['pipe'=2,'dp'=4,'rows'=4] {'dp','rows'}, use_global_device_ids=true, to_apply=%region_104.105 | all-reduce | flops 1024 | bytes 8192 | tf_op jit(solution)/shard_map/psum | solution.py:209
  2199.3 6.2 convolution_bitcast_fusion.1
  2205.4 37.9 %fusion.3 = f32[1,2,4608,512]{3,2,1,0:T(8,128)} fusion(f32[1,1,4608,512]{3,2,1,0:T(8,128)} %convolution_bitcast_fusion.8, f32[1,1,4608,512]{3,2,1,0:T(8,128)} %convolution_bitcast_fusion.9, f32[1,1,4608,512]{3,2,1,0:T(8,128)} %convolution_bitcast_fusion.6, f32[1,1,4608,512]{3,2,1,0:T(8,128)} %convolution_bitcast_fusion.7, ...), kind=kLoop, calls=%fused_computation.8 | loop fusion | flops 42467328 | bytes 113246208 | tf_op jit(solution)/shard_map/add | solution.py:386
  2269.6 11.4 fusion.55
  2287.9 11.5 fusion.57
  2302.9 11.3 fusion.51
  2314.2 11.4 fusion.53
  2325.6 45.4 %fusion = f32[1,3,4608,512]{3,2,1,0:T(8,128)} fusion(f32[3,4608,512,1]{2,1,3,0:T(8,128)} %fusion.51, f32[3,4608,512,1]{2,1,3,0:T(8,128)} %fusion.53, f32[3,4608,512,1]{2,1,3,0:T(8,128)} %fusion.55, f32[3,4608,512,1]{2,1,3,0:T(8,128)} %fusion.57, bf16[3,1,2,32,4608]{4,3,2,0,1:T(8,128)(2,1)S(1)} %constant_dynamic-update-slice_fusion.468, ...), kind=kOutput, calls=%fused_computation.1 | convolution fusion | flops 934674432 | bytes 143720960 | tf_op jit(solution)/shard_map/ksrwq,ksrwd->kqd/dot_general | solution.py:102
  2395.8 7.6 fusion.145
  2405.9 76.2 %reduce-scatter.12.cloned.1.call-done = f32[1,3,32,128]{3,2,1,0:T(8,128)} async-done(((f32[1,3,512,128]{3,2,1,0:T(8,128)}), f32[1,3,32,128]{3,2,1,0:T(8,128)}) %reduce-scatter.12.cloned.1.call-update) | async-done | bytes 49168 | tf_op jit(solution)/shard_map/reduce_scatter | solution.py:418
  2482.1 288.5 %reduce-scatter.10.cloned.1.call-done = f32[1,2,288,512]{3,2,1,0:T(8,128)} async-done(((f32[1,2,4608,512]{3,2,1,0:T(8,128)}), f32[1,2,288,512]{3,2,1,0:T(8,128)}) %reduce-scatter.10.cloned.1.call-update) | async-done | bytes 1179664 | tf_op jit(solution)/shard_map/reduce_scatter | solution.py:415
  2770.5 405.5 %reduce-scatter.14.cloned.1.call-done = f32[1,3,288,512]{3,2,1,0:T(8,128)} async-done(((f32[1,3,4608,512]{3,2,1,0:T(8,128)}), f32[1,3,288,512]{3,2,1,0:T(8,128)}) %reduce-scatter.14.cloned.1.call-update) | async-done | bytes 1769488 | tf_op jit(solution)/shard_map/reduce_scatter | solution.py:420
  (1694 shorter events, 646.6 us)
Async XLA Ops:
  7.2 248.8 %all-gather.3.cloned.1.call-start = ((), (), s32[]{:S(2)}) async-start(), calls=%async_computation.5 | async-start | bytes 10027008 | tf_op jit(solution)/shard_map/all_gather | solution.py:291
  7.9 432.1 %all-gather.5.cloned.1.call-start = ((), (), s32[]{:S(2)}) async-start(), calls=%async_computation.6 | async-start | bytes 15040512 | tf_op jit(solution)/shard_map/all_gather | solution.py:296
  8.7 2378.9 %reduce-scatter.16.cloned.1.call-start = ((), (), s32[]{:S(2)}) async-start(), calls=%async_computation.10 | async-start | bytes 278528
  11.2 217.0 %collective-permute-start.1 = (bf16[1,1,1,32,512]{4,3,2,1,0:T(8,128)(2,1)}, bf16[1,1,1,32,512]{4,3,2,1,0:T(8,128)(2,1)S(1)}, u32[]{:S(2)}, u32[]{:S(2)}) collective-permute-start(bf16[1,1,1,32,512]{4,3,2,1,0:T(8,128)(2,1)} %get-tuple-element.287), channel_id=1, source_target_pairs={{1,0},{2,1},{3,2},{5,4},{6,5},{7,6},{9,8},{10,9},{11,10},{13,12},{... | collective-permute-start | bytes 98312 | tf_op jit(solution)/shard_map/ppermute | solution.py:20
  12.5 217.1 %collective-permute-start = (bf16[1,1,1,32,512]{4,3,2,1,0:T(8,128)(2,1)}, bf16[1,1,1,32,512]{4,3,2,1,0:T(8,128)(2,1)S(1)}, u32[]{:S(2)}, u32[]{:S(2)}) collective-permute-start(bf16[1,1,1,32,512]{4,3,2,1,0:T(8,128)(2,1)} %get-tuple-element.286), channel_id=1, source_target_pairs={{0,1},{1,2},{2,3},{4,5},{5,6},{6,7},{8,9},{9,10},{10,11},{12,13},{... | collective-permute-start | bytes 98312 | tf_op jit(solution)/shard_map/ppermute | solution.py:19
  19.3 211.8 %collective-permute-start.35 = (bf16[3,1,1,32,512]{4,3,2,0,1:T(8,128)(2,1)}, bf16[3,1,1,32,512]{4,3,2,0,1:T(8,128)(2,1)S(1)}, u32[]{:S(2)}, u32[]{:S(2)}) collective-permute-start(bf16[3,1,1,32,512]{4,3,2,0,1:T(8,128)(2,1)} %get-tuple-element.185), channel_id=1, source_target_pairs={{1,0},{2,1},{3,2},{5,4},{6,5},{7,6},{9,8},{10,9},{11,10},{13,12},{... | collective-permute-start | bytes 294920 | tf_op jit(solution)/shard_map/ppermute | solution.py:20
  20.6 215.1 %collective-permute-start.34 = (bf16[3,1,1,32,512]{4,3,2,0,1:T(8,128)(2,1)}, bf16[3,1,1,32,512]{4,3,2,0,1:T(8,128)(2,1)S(1)}, u32[]{:S(2)}, u32[]{:S(2)}) collective-permute-start(bf16[3,1,1,32,512]{4,3,2,0,1:T(8,128)(2,1)} %get-tuple-element.184), channel_id=1, source_target_pairs={{0,1},{1,2},{2,3},{4,5},{5,6},{6,7},{8,9},{9,10},{10,11},{12,13},{... | collective-permute-start | bytes 294920 | tf_op jit(solution)/shard_map/ppermute | solution.py:19
  25.9 212.9 %collective-permute-start.41 = (bf16[3,1,1,32,512]{4,3,2,0,1:T(8,128)(2,1)}, bf16[3,1,1,32,512]{4,3,2,0,1:T(8,128)(2,1)S(1)}, u32[]{:S(2)}, u32[]{:S(2)}) collective-permute-start(bf16[3,1,1,32,512]{4,3,2,0,1:T(8,128)(2,1)} %get-tuple-element.187), channel_id=1, source_target_pairs={{1,0},{2,1},{3,2},{5,4},{6,5},{7,6},{9,8},{10,9},{11,10},{13,12},{... | collective-permute-start | bytes 294920 | tf_op jit(solution)/shard_map/ppermute | solution.py:20
  228.3 15.2 collective-permute-start.40
  229.6 14.1 collective-permute-start.47
  231.1 12.6 collective-permute-start.46
  337.8 14.0 collective-permute-start.3
  339.1 12.7 collective-permute-start.2
  448.3 39.5 %collective-permute-start.6 = (bf16[4,1,1,16,512]{4,3,2,1,0:T(8,128)(2,1)S(1)}, bf16[4,1,1,16,512]{4,3,2,1,0:T(8,128)(2,1)S(1)}, u32[]{:S(2)}, u32[]{:S(2)}) collective-permute-start(bf16[4,1,1,16,512]{4,3,2,1,0:T(8,128)(2,1)S(1)} %pad_maximum_fusion.89), channel_id=1, source_target_pairs={{0,16},{1,17},{2,18},{3,19},{4,20},{5,21},{6,22},{7,23},{8,24},{9,... | collective-permute-start | bytes 196616 | tf_op jit(solution)/shard_map/ppermute | solution.py:28
  684.3 300.1 %collective-permute-start.37 = (bf16[1,1,1,32,512]{4,3,2,1,0:T(8,128)(2,1)}, bf16[1,1,1,32,512]{4,3,2,1,0:T(8,128)(2,1)S(1)}, u32[]{:S(2)}, u32[]{:S(2)}) collective-permute-start(bf16[1,1,1,32,512]{4,3,2,1,0:T(8,128)(2,1)} %get-tuple-element.263), channel_id=1, source_target_pairs={{1,0},{2,1},{3,2},{5,4},{6,5},{7,6},{9,8},{10,9},{11,10},{13,12},{... | collective-permute-start | bytes 98312 | tf_op jit(solution)/shard_map/ppermute | solution.py:20
  685.6 303.4 %collective-permute-start.36 = (bf16[1,1,1,32,512]{4,3,2,1,0:T(8,128)(2,1)}, bf16[1,1,1,32,512]{4,3,2,1,0:T(8,128)(2,1)S(1)}, u32[]{:S(2)}, u32[]{:S(2)}) collective-permute-start(bf16[1,1,1,32,512]{4,3,2,1,0:T(8,128)(2,1)} %get-tuple-element.262), channel_id=1, source_target_pairs={{0,1},{1,2},{2,3},{4,5},{5,6},{6,7},{8,9},{9,10},{10,11},{12,13},{... | collective-permute-start | bytes 98312 | tf_op jit(solution)/shard_map/ppermute | solution.py:19
  884.7 106.2 %collective-permute-start.43 = (bf16[1,1,1,32,512]{4,3,2,1,0:T(8,128)(2,1)S(1)}, bf16[1,1,1,32,512]{4,3,2,1,0:T(8,128)(2,1)S(1)}, u32[]{:S(2)}, u32[]{:S(2)}) collective-permute-start(bf16[1,1,1,32,512]{4,3,2,1,0:T(8,128)(2,1)S(1)} %get-tuple-element.259), channel_id=1, source_target_pairs={{1,0},{2,1},{3,2},{5,4},{6,5},{7,6},{9,8},{10,9},{11,10},{13,12},{... | collective-permute-start | bytes 98312 | tf_op jit(solution)/shard_map/ppermute | solution.py:20
  889.2 9.5 collective-permute-start.22
  890.5 12.1 collective-permute-start.21
  898.7 96.8 %collective-permute-start.42 = (bf16[1,1,1,32,512]{4,3,2,1,0:T(8,128)(2,1)S(1)}, bf16[1,1,1,32,512]{4,3,2,1,0:T(8,128)(2,1)S(1)}, u32[]{:S(2)}, u32[]{:S(2)}) collective-permute-start(bf16[1,1,1,32,512]{4,3,2,1,0:T(8,128)(2,1)S(1)} %get-tuple-element.258), channel_id=1, source_target_pairs={{0,1},{1,2},{2,3},{4,5},{5,6},{6,7},{8,9},{9,10},{10,11},{12,13},{... | collective-permute-start | bytes 98312 | tf_op jit(solution)/shard_map/ppermute | solution.py:19
  902.6 92.9 %collective-permute-start.49 = (bf16[1,1,1,32,512]{4,3,2,1,0:T(8,128)(2,1)S(1)}, bf16[1,1,1,32,512]{4,3,2,1,0:T(8,128)(2,1)S(1)}, u32[]{:S(2)}, u32[]{:S(2)}) collective-permute-start(bf16[1,1,1,32,512]{4,3,2,1,0:T(8,128)(2,1)S(1)} %get-tuple-element.255), channel_id=1, source_target_pairs={{1,0},{2,1},{3,2},{5,4},{6,5},{7,6},{9,8},{10,9},{11,10},{13,12},{... | collective-permute-start | bytes 98312 | tf_op jit(solution)/shard_map/ppermute | solution.py:20
  985.0 10.4 collective-permute-start.48
  989.6 16.1 collective-permute-start.24
  990.9 14.8 collective-permute-start.23
  1103.8 14.3 collective-permute-start.55
  1105.1 13.0 collective-permute-start.54
  1110.1 9.2 collective-permute-start.29
  1207.6 13.8 collective-permute-start.39
  1209.0 17.0 collective-permute-start.38
  1214.0 13.3 collective-permute-start.45
  1215.3 16.6 collective-permute-start.44
  1219.9 13.3 collective-permute-start.51
  1221.4 16.3 collective-permute-start.50
  1226.0 13.8 collective-permute-start.57
  1227.3 12.5 collective-permute-start.56
  1560.7 14.6 collective-permute-start.61
  1562.0 13.3 collective-permute-start.60
  1646.1 12.2 collective-permute-start.66
  1647.3 10.9 collective-permute-start.65
  1714.6 13.3 collective-permute-start.68
  1715.9 12.0 collective-permute-start.67
  1791.9 10.7 collective-permute-start.73
  1793.2 9.4 collective-permute-start.72
  1859.5 12.6 collective-permute-start.75
  1860.8 11.3 collective-permute-start.74
  1995.1 14.5 collective-permute-start.82
  1996.4 13.2 collective-permute-start.81
  2141.2 247.8 %reduce-scatter.18.cloned.1.call-start = ((), (), s32[]{:S(2)}) async-start(), calls=%async_computation.11 | async-start | bytes 278528
  2142.3 262.2 %all-reduce.59.cloned.1.call-start = ((), (), s32[]{:S(2)}) async-start(), calls=%async_computation.12 | async-start | bytes 1572864
  2148.6 333.5 %reduce-scatter.12.cloned.1.call-start = ((), (), s32[]{:S(2)}) async-start(), calls=%async_computation.8 | async-start | bytes 835584 | tf_op jit(solution)/shard_map/reduce_scatter | solution.py:418
  2160.4 610.2 %reduce-scatter.10.cloned.1.call-start = ((), (), s32[]{:S(2)}) async-start(), calls=%async_computation.7 | async-start | bytes 20054016 | tf_op jit(solution)/shard_map/reduce_scatter | solution.py:415
  2243.5 932.6 %reduce-scatter.14.cloned.1.call-start = ((), (), s32[]{:S(2)}) async-start(), calls=%async_computation.9 | async-start | bytes 30081024 | tf_op jit(solution)/shard_map/reduce_scatter | solution.py:420
  2245.7 14.6 collective-permute-start.93
  2247.0 18.5 collective-permute-start.92
  2252.5 13.1 collective-permute-start.95
  2253.8 12.4 collective-permute-start.94
  2259.0 40.6 %collective-permute-start.97 = (bf16[3,1,1,32,512]{4,3,2,0,1:T(8,128)(2,1)}, bf16[3,1,1,32,512]{4,3,2,0,1:T(8,128)(2,1)}, u32[]{:S(2)}, u32[]{:S(2)}) collective-permute-start(bf16[3,1,1,32,512]{4,3,2,0,1:T(8,128)(2,1)} %get-tuple-element.173), channel_id=1, source_target_pairs={{1,0},{2,1},{3,2},{5,4},{6,5},{7,6},{9,8},{10,9},{11,10},{13,12},{... | collective-permute-start | bytes 294920 | tf_op jit(solution)/shard_map/ppermute | solution.py:20
  2260.3 39.3 %collective-permute-start.96 = (bf16[3,1,1,32,512]{4,3,2,0,1:T(8,128)(2,1)}, bf16[3,1,1,32,512]{4,3,2,0,1:T(8,128)(2,1)}, u32[]{:S(2)}, u32[]{:S(2)}) collective-permute-start(bf16[3,1,1,32,512]{4,3,2,0,1:T(8,128)(2,1)} %get-tuple-element.172), channel_id=1, source_target_pairs={{0,1},{1,2},{2,3},{4,5},{5,6},{6,7},{8,9},{9,10},{10,11},{12,13},{... | collective-permute-start | bytes 294920 | tf_op jit(solution)/shard_map/ppermute | solution.py:19
  2281.7 18.0 collective-permute-start.99
  2283.0 16.7 collective-permute-start.98
  2375.6 14.8 collective-permute-start.91
  2376.9 13.5 collective-permute-start.90
  2381.4 13.9 collective-permute-start.33
  2382.7 12.6 collective-permute-start.32
  (332 other events, 6755.1 us)
Sparse Core Ops, SparseCore 0:
  10.9 138.7 all-gather.2
  152.5 175.0 all-gather.4
  2141.3 74.1 reduce-scatter.15
  2217.7 73.0 reduce-scatter.17
  2295.9 106.5 all-reduce.58
  2405.2 76.7 reduce-scatter.11
  2489.4 281.1 reduce-scatter.9
  2777.9 398.1 reduce-scatter.13
where the time goes:
time: 3200 us; the launch traced here: 3180 us
  blocking collectives  1370 us (43%)
  waiting for transfers between devices  792 us (25%)
  matrix products  397 us (12%)
  starting transfers between devices  286 us (9%)
  between operations  119 us (4%)
  other arithmetic  114 us (4%)
  local copies, waits for them, and re-layouts  109 us (3%)
    reduce_scatter x1, waiting for transfers between devices, on_device(): lax.psum_scatter(task_sum[None], ('dp', 'rows'), scatter_dimension=2, til...  406 us
    psum x10, blocking collectives, norm_moments(): lax.psum(jnp.sum(conv_out, axis=(0, 1, 2, 3)), ('dp', 'rows')) / pixel_count  390 us
    psum x10, blocking collectives, trunk_backward(): bias_total, gain_total = lax.psum((bias_part, gain_part), ('dp', 'rows'))  386 us
    psum x10, blocking collectives, norm_moments(): lax.psum(jnp.sum(jnp.square(conv_out - center), axis=(0, 1, 2, 3)), ('dp'...  371 us
    reduce_scatter x1, waiting for transfers between devices, on_device(): lax.psum_scatter(trunk_sum[None], ('dp', 'rows'), scatter_dimension=2, ti...  288 us
    ppermute x46, starting transfers between devices, extended_2(): before = lax.ppermute(last, axis, up)  216 us
    dot_general x15, matrix products, conv_backward(): jnp.einsum('ksrwq,ksrwd->kqd', gather_taps(padded, rows_n, cols_n), grad_...  150 us
    dot_general x19, matrix products, conv_backward(): jnp.einsum('ksrwtd,ktcd->ksrwc', flipped, kernel, preferred_element_type=...  112 us
  transfers between devices with their start and end apart: 108, of which 23 were waited for; matrix products, arithmetic and copies ran while one was open for 12% of the time, Pallas kernels for 0%

commit v1 on v0

--- a/solution.py
+++ b/solution.py
@@ -1,6 +1,10 @@
+import functools
+
 import jax
 import jax.numpy as jnp
 from jax import lax
+from jax.experimental import pallas as pl
+from jax.experimental.pallas import tpu as pltpu
 from jax.sharding import PartitionSpec as P
 
 NASH_ITERS = 3
@@ -432,6 +436,1367 @@
     )
 
 
+BF = jnp.bfloat16
+F32 = jnp.float32
+LANES = 128
+TAPS = 9
+VMEM_BYTES = 56 * 1024 * 1024
+
+
+class Line:
+    def __init__(self, ids):
+        self.ids = ids
+        self.last = None
+
+
+def on_section(body, only):
+    if only is None:
+        return body
+
+    def gated(ids_ref, *refs):
+        @pl.when(ids_ref[2] == only)
+        def _():
+            body(ids_ref, *refs)
+
+    return gated
+
+
+def unread(body, count, first):
+    def whole(*refs):
+        body(*refs[:first], *refs[first + count :])
+
+    return whole
+
+
+LIGHT = pl.CostEstimate(flops=300_000_000, bytes_accessed=1, transcendentals=0)
+
+
+def kernel_call(body, outs, line, vmem, name, scratch=(), only=None, smem=(), after=()):
+    extra = list(after) + ([] if line.last is None else [line.last])
+    first = 1 + len(smem) + len(vmem)
+    results = pl.pallas_call(
+        unread(on_section(body, only), len(extra), first),
+        out_shape=[jax.ShapeDtypeStruct(shape, dtype) for shape, dtype in outs],
+        in_specs=[pl.BlockSpec(memory_space=pltpu.SMEM)] * (1 + len(smem))
+        + [pl.BlockSpec(memory_space=pltpu.VMEM)] * len(vmem)
+        + [pl.BlockSpec(memory_space=pl.ANY)] * len(extra),
+        out_specs=[pl.BlockSpec(memory_space=pltpu.VMEM)] * len(outs),
+        scratch_shapes=list(scratch),
+        compiler_params=pltpu.CompilerParams(vmem_limit_bytes=VMEM_BYTES),
+        cost_estimate=LIGHT,
+        name=name,
+    )(line.ids, *smem, *vmem, *extra)
+    line.last = results[-1]
+    return results
+
+
+def stepped_call(body, outs, line, vmem, name, scratch=(), only=None, fixed=()):
+    extra = [] if line.last is None else [line.last]
+    steps = outs[0][0][0]
+
+    def block(shape):
+        rest = len(shape) - 1
+        return pl.BlockSpec(
+            (1,) + tuple(shape[1:]),
+            lambda t, ids: (t if only is None else jnp.where(ids[2] == only, t, 0),) + (0,) * rest,
+        )
+
+    def same(shape):
+        return pl.BlockSpec(shape, lambda t, ids: (0,) * len(shape))
+
+    results = pl.pallas_call(
+        unread(on_section(body, only), len(extra), 1 + len(vmem)),
+        grid_spec=pltpu.PrefetchScalarGridSpec(
+            num_scalar_prefetch=1,
+            grid=(steps,),
+            in_specs=[same(a.shape) if k in fixed else block(a.shape) for k, a in enumerate(vmem)]
+            + [pl.BlockSpec(memory_space=pl.ANY)] * len(extra),
+            out_specs=[block(shape) for shape, _ in outs],
+            scratch_shapes=list(scratch),
+        ),
+        out_shape=[jax.ShapeDtypeStruct(shape, dtype) for shape, dtype in outs],
+        compiler_params=pltpu.CompilerParams(vmem_limit_bytes=VMEM_BYTES),
+        cost_estimate=LIGHT,
+        name=name,
+    )(line.ids, *vmem, *extra)
+    line.last = results[-1]
+    return results
+
+
+class Parts:
+    def __init__(self, given, held, given_sems, results, kept, result_sems, split_in, split_out):
+        self.given = [self.copies(a, b, given_sems, k, k in split_in) for k, (a, b) in enumerate(zip(given, held))]
+        self.results = [
+            self.copies(b, a, result_sems, k, k in split_out) for k, (a, b) in enumerate(zip(results, kept))
+        ]
+        self.waiting = []
+
+    def copies(self, source, target, sems, k, split):
+        if not split:
+            return [pltpu.make_async_copy(source, target, sems.at[k, 0])]
+        return [
+            pltpu.make_async_copy(source.at[p], target.at[p], sems.at[k, p])
+            for p in range(source.shape[0])
+        ]
+
+    def begin(self):
+        for p in range(3):
+            for copies in self.given:
+                if p < len(copies):
+                    copies[p].start()
+
+    def need(self, k, p=0):
+        self.given[k][p].wait()
+
+    def send(self, k, p=0):
+        self.results[k][p].start()
+        self.waiting.append(self.results[k][p])
+
+    def finish(self):
+        for copy in self.waiting:
+            copy.wait()
+
+
+def section_call(
+    body, outs, line, vmem, name, scratch=(), only=None, other=None, paired=(), split_in=(), split_out=(), smem=()
+):
+    other, paired = dict(other or {}), dict(paired)
+    n_in, n_out = len(vmem), len(outs)
+    passed, swapped = list(other.values()), list(paired.values())
+    extra = [] if line.last is None else [line.last]
+
+    def whole(*refs):
+        scalars, refs = refs[: 1 + len(smem)], refs[1 + len(smem) :]
+        ids_ref = scalars[0]
+        given, refs = refs[:n_in], refs[n_in:]
+        passed_refs, refs = refs[: len(passed)], refs[len(passed) :]
+        swapped_refs, refs = refs[: len(swapped)], refs[len(swapped) + len(extra) :]
+        results, refs = refs[:n_out], refs[n_out:]
+        held, refs = refs[:n_in], refs[n_in:]
+        kept, refs = refs[:n_out], refs[n_out:]
+        given_sems, result_sems, refs = refs[0], refs[1], refs[2:]
+
+        def run(sources):
+            parts = Parts(sources, held, given_sems, results, kept, result_sems, split_in, split_out)
+            parts.begin()
+            for k in range(n_in):
+                if k not in split_in:
+                    parts.need(k)
+            if split_in or split_out:
+                body(*scalars, *held, *kept, *refs, parts=parts)
+            else:
+                body(*scalars, *held, *kept, *refs)
+            for k in range(n_out):
+                if k not in split_out:
+                    parts.send(k)
+            parts.finish()
+
+        def hand_out():
+            for source, target in ((passed_refs, kept), (kept, results)):
+                copies = []
+                for at, k in enumerate(other):
+                    first = source[at] if source is passed_refs else source[k]
+                    copies.append(pltpu.make_async_copy(first, target[k], result_sems.at[k, 0]))
+                for copy in copies:
+                    copy.start()
+                for copy in copies:
+                    copy.wait()
+
+        if only is not None:
+            pl.when(ids_ref[2] == only)(lambda: run(given))
+            if passed:
+                pl.when(ids_ref[2] != only)(hand_out)
+        elif paired:
+            mixed = list(given)
+            for k, ref in zip(paired, swapped_refs):
+                mixed[k] = ref
+            pl.when(ids_ref[2] == 0)(lambda: run(given))
+            pl.when(ids_ref[2] == 1)(lambda: run(mixed))
+        else:
+            run(given)
+
+    results = pl.pallas_call(
+        whole,
+        out_shape=[jax.ShapeDtypeStruct(shape, dtype) for shape, dtype in outs],
+        in_specs=[pl.BlockSpec(memory_space=pltpu.SMEM)] * (1 + len(smem))
+        + [pl.BlockSpec(memory_space=pl.ANY)] * (n_in + len(passed) + len(swapped) + len(extra)),
+        out_specs=[pl.BlockSpec(memory_space=pl.ANY)] * n_out,
+        scratch_shapes=[pltpu.VMEM(a.shape, a.dtype) for a in vmem]
+        + [pltpu.VMEM(shape, dtype) for shape, dtype in outs]
+        + [pltpu.SemaphoreType.DMA((n_in, 3)), pltpu.SemaphoreType.DMA((n_out, 3))]
+        + list(scratch),
+        compiler_params=pltpu.CompilerParams(vmem_limit_bytes=VMEM_BYTES),
+        cost_estimate=LIGHT,
+        name=name,
+    )(line.ids, *smem, *vmem, *passed, *swapped, *extra)
+    line.last = results[-1]
+    return results
+
+
+def anchor(line, arrays, name):
+    def body(*refs):
+        refs[-1][...] = jnp.zeros((8, LANES), F32)
+
+    line.last = pl.pallas_call(
+        body,
+        out_shape=jax.ShapeDtypeStruct((8, LANES), F32),
+        in_specs=[pl.BlockSpec(memory_space=pl.ANY)] * (len(arrays) + 1),
+        out_specs=pl.BlockSpec(memory_space=pltpu.VMEM),
+        cost_estimate=LIGHT,
+        name=name,
+    )(*arrays, line.last)
+
+
+def trade(pieces, axis, sections):
+    count = lax.axis_size(axis)
+    taken = [pieces[0]]
+    for j in range(1, count):
+        pairs = [(p * count + i, p * count + (i ^ j)) for p in sections for i in range(count)]
+        taken.append(lax.ppermute(pieces[j], ("pipe", axis), pairs))
+    return taken
+
+
+def swap_sections(pieces):
+    count = lax.axis_size("dp")
+    return [
+        lax.ppermute(
+            pieces[j],
+            ("pipe", "dp"),
+            [(p * count + i, (1 - p) * count + (i ^ j)) for p in range(2) for i in range(count)],
+        )
+        for j in range(len(pieces))
+    ]
+
+
+def span(index, size):
+    return pl.ds(pl.multiple_of(index * size, size), size)
+
+
+def dot(a, b):
+    return jnp.dot(a, b, preferred_element_type=F32)
+
+
+def dot_nt(a, b):
+    return lax.dot_general(a, b, (((1,), (1,)), ((), ())), preferred_element_type=F32)
+
+
+def dot_tn(a, b):
+    return lax.dot_general(a, b, (((0,), (0,)), ((), ())), preferred_element_type=F32)
+
+
+def column_of(shape, cols):
+    return lax.broadcasted_iota(jnp.int32, shape, 0) % cols
+
+
+def fold_taps(taps, cols):
+    size = taps.shape[0]
+    blank = jnp.zeros((cols, LANES), F32)
+    sums = []
+    for b in range(3):
+        first = taps[:, b * LANES : (b + 1) * LANES]
+        second = taps[:, (3 + b) * LANES : (4 + b) * LANES]
+        third = taps[:, (6 + b) * LANES : (7 + b) * LANES]
+        sums.append(
+            second
+            + jnp.concatenate([blank, first[: size - cols]], axis=0)
+            + jnp.concatenate([third[cols:], blank], axis=0)
+        )
+    column = column_of((size, LANES), cols)
+    left = jnp.where(column == 0, 0.0, pltpu.roll(sums[0], 1, 0))
+    right = jnp.where(column == cols - 1, 0.0, pltpu.roll(sums[2], size - 1, 0))
+    return sums[1] + left + right
+
+
+def spread_taps(grad, cols):
+    size = grad.shape[0]
+    column = column_of((size, LANES), cols)
+    moved = [
+        jnp.where(column == cols - 1, 0.0, pltpu.roll(grad, size - 1, 0)).astype(BF),
+        grad.astype(BF),
+        jnp.where(column == 0, 0.0, pltpu.roll(grad, 1, 0)).astype(BF),
+    ]
+    blank = jnp.zeros((cols, LANES), BF)
+    above = [jnp.concatenate([m[cols:], blank], axis=0) for m in moved]
+    below = [jnp.concatenate([blank, m[: size - cols]], axis=0) for m in moved]
+    return jnp.concatenate(above + moved + below, axis=1)
+
+
+def cut_weights(line, arrays, name):
+    depth = arrays[0][0].shape[1]
+    count = sum(len(layers) for _, layers in arrays)
+
+    def body(ids_ref, *refs):
+        given, outs = refs[: len(arrays)], refs[len(arrays) :]
+        for j in range(4):
+            cut = span(ids_ref[0] ^ j, LANES)
+            row = 0
+            for ref, (_, layers) in zip(given, arrays):
+                for n in layers:
+                    outs[j][row * depth : (row + 1) * depth, :] = ref[n, :, cut]
+                    row += 1
+
+    return kernel_call(
+        body, [((count * depth, LANES), BF)] * 4, line, [a for a, _ in arrays], name
+    )
+
+
+def stack_weights(line, pieces, groups, extra, name):
+    depth = pieces[0].shape[0] // sum(len(group) for group in groups)
+    more = [a for arrays in extra for a in arrays]
+
+    def body(ids_ref, *refs):
+        given, more_in, outs = refs[:4], list(refs[4 : 4 + len(more)]), refs[4 + len(more) :]
+        for k, group in enumerate(groups):
+            for at, n in enumerate(group):
+                for j in range(4):
+                    rows = span(4 * at + (ids_ref[0] ^ j), depth)
+                    outs[k][rows, :] = given[j][n * depth : (n + 1) * depth, :]
+            at = 4 * len(group) * depth
+            for array in extra[k]:
+                outs[k][at : at + array.shape[0], :] = more_in.pop(0)[...]
+                at += array.shape[0]
+
+    sizes = [
+        4 * len(group) * depth + sum(a.shape[0] for a in extra[k])
+        for k, group in enumerate(groups)
+    ]
+    return kernel_call(
+        body, [((n, LANES), BF) for n in sizes], line, list(pieces) + more, name
+    )
+
+
+def place_weights(line, gathered, count, depth, name, norm_rows=0, tail_rows=0):
+    whole = 16 * depth
+    channels = whole // TAPS
+    end = 4 * count * depth
+    apart = norm_rows > 0
+
+    def body(ids_ref, g_ref, *rest):
+        flat = rest[-1]
+        for n in range(count):
+            for r in range(4):
+                for p in range(4):
+                    rows = slice((4 * n + p) * depth, (4 * n + p + 1) * depth)
+                    flat[(p * 4 + r) * depth : (p * 4 + r + 1) * depth, :] = g_ref[r, rows, :]
+            for tap in range(TAPS):
+                lanes = slice(tap * LANES, (tap + 1) * LANES)
+                value = flat[tap * channels : (tap + 1) * channels, :]
+                if apart:
+                    rest[n][0, :, lanes] = value
+                else:
+                    rest[0][n, :, lanes] = value
+        if apart:
+            own = [g_ref[r, end : end + norm_rows, :].astype(F32) for r in range(4)]
+            rest[count][...] = (own[0] + own[1]) + (own[2] + own[3])
+            rest[count + 1][...] = g_ref[:, end + norm_rows : end + norm_rows + tail_rows, :]
+
+    if apart:
+        outs = [((1, channels, TAPS * LANES), BF)] * count
+        outs += [((norm_rows, LANES), F32), ((4, tail_rows, LANES), BF)]
+    else:
+        outs = [((count, channels, TAPS * LANES), BF)]
+    return kernel_call(
+        body, outs, line, [gathered], name, scratch=[pltpu.VMEM((whole, LANES), BF)]
+    )
+
+
+def place_attention(line, pieces, maps, part):
+    def body(ids_ref, *refs):
+        given, out = refs[:4], refs[4]
+        for j in range(4):
+            for r in range(4):
+                chunk = (ids_ref[0] ^ j) * 4 + r
+                for t in range(maps):
+                    out[t, span(chunk, part), :] = given[j][r, t * part : (t + 1) * part, :]
+
+    return kernel_call(
+        body, [((maps, 16 * part, LANES), BF)], line, list(pieces), "place_attention"
+    )[0]
+
+
+def trunk_layer(
+    line, pieces, weight, norms, layer, cols, eps_value, form, last, masked, name, only=None
+):
+    channels = weight.shape[1]
+    size = {"images": 1, "slices": 0.25, "cells": 1}[form]
+    size = int(pieces[0].shape[0] * size)
+    pixels = 4 * size
+    whole_images = form == "images"
+
+    def body(ids_ref, *refs):
+        given, (w_ref, norm_ref) = refs[:4], refs[4:6]
+        at = 6
+        if masked is not None and not whole_images:
+            mask_ref = refs[6]
+            at = 7
+        outs, v_ref, pairs_ref = refs[at:-2], refs[-2], refs[-1]
+        field = outs[0]
+        for j in range(4):
+            peer = ids_ref[0] ^ j
+            if whole_images:
+                field[span(peer, size), :] = given[j][:, :channels]
+                outs[4][span(peer, size), :] = given[j][:, channels:]
+            elif form == "cells":
+                cells = spread_pairs(given[j][...].astype(F32), pairs_ref, cols)
+                field[:, span(peer, LANES)] = cells.astype(BF) * mask_ref[...]
+            else:
+                field[:, span(peer, LANES)] = given[j][...]
+        for i in range(4):
+            part = slice(i * size, (i + 1) * size)
+            v_ref[part, :] = fold_taps(dot(field[part, :], w_ref[0]), cols)
+        conv_out = v_ref[...]
+        center = jnp.sum(conv_out, axis=0, keepdims=True) / pixels
+        moved = conv_out - center
+        spread = jnp.sum(moved * moved, axis=0, keepdims=True) / pixels
+        inverse = lax.rsqrt(spread + eps_value)
+        normed = moved * inverse
+        outs[1][...] = normed
+        outs[2][...] = jnp.broadcast_to(inverse, (8, LANES))
+        preact = norm_ref[layer : layer + 1, :] * normed + norm_ref[2 + layer : 3 + layer, :]
+        hidden = (preact * jax.nn.sigmoid(preact)).astype(BF)
+        outs[3][...] = hidden
+        if last and masked is not None:
+            kept = hidden.astype(F32) * mask_ref[...].astype(F32)
+            outs[4][...] = pool_pairs(kept, pairs_ref, cols).astype(BF)
+
+    outs = [((pixels, channels), BF), ((pixels, LANES), F32), ((8, LANES), F32)]
+    outs.append(((pixels, LANES), BF))
+    if last and masked is not None:
+        outs.append(((size, LANES), BF))
+    elif whole_images:
+        outs.append(((pixels, LANES), BF))
+    extra = [masked] if masked is not None and not whole_images else []
+    return kernel_call(
+        body,
+        outs,
+        line,
+        list(pieces) + [weight, norms] + extra,
+        name,
+        scratch=[pltpu.VMEM((pixels, LANES), F32), pltpu.VMEM((pixels // 2, LANES), F32)],
+        only=only,
+    )
+
+
+def pool_pairs(value, pairs_ref, cols):
+    size = value.shape[0]
+    halves = value.reshape(size // (2 * cols), 2, cols, LANES)
+    pairs_ref[: size // 2, :] = (halves[:, 0] + halves[:, 1]).reshape(size // 2, LANES)
+    return pairs_ref[pl.ds(0, size // 4, stride=2), :] + pairs_ref[pl.ds(1, size // 4, stride=2), :]
+
+
+def spread_pairs(small, pairs_ref, cols):
+    size = 4 * small.shape[0]
+    pairs_ref[pl.ds(0, size // 4, stride=2), :] = small
+    pairs_ref[pl.ds(1, size // 4, stride=2), :] = small
+    rows = pairs_ref[: size // 2, :].reshape(size // (2 * cols), 1, cols, LANES)
+    return jnp.broadcast_to(rows, (size // (2 * cols), 2, cols, LANES)).reshape(size, LANES)
+
+
+def attend(x, mixture, down, up_t):
+    inner = dot(mixture, down)
+    active = (inner * jax.nn.sigmoid(inner)).astype(BF)
+    gate = jax.nn.sigmoid(dot_nt(active, up_t))
+    return inner, active, gate
+
+
+def label_at(label_ref, ids_ref, device, t):
+    return label_ref[(device * 4 + ids_ref[1]) * 3 + t]
+
+
+def slot_of(label_ref, ids_ref, device, t):
+    return sum([label_at(label_ref, ids_ref, device, k) for k in range(t)], jnp.int32(0))
+
+
+def section_tasks(line, labels, x_slices, att, weights, mask, cots, cols):
+    pixels = x_slices[0].shape[0]
+    size = pixels // 4
+    tasks_n, channels, _ = weights.shape
+    down, up_t = att[:tasks_n], att[tasks_n:]
+
+    def body(ids_ref, label_ref, *refs):
+        x_in, down_ref, up_ref, w_ref, mask_ref, cot_in = refs[:4], *refs[4:8], refs[8:12]
+        fields, feats, cells, du = refs[12:16], refs[16:20], refs[20], refs[21:25]
+        x_ref, pairs_ref = refs[25:]
+        t = pl.program_id(0)
+
+        @pl.when(ids_ref[2] == 0)
+        def _():
+            @pl.when(t == 0)
+            def _():
+                for j in range(4):
+                    x_ref[:, span(ids_ref[0] ^ j, LANES)] = x_in[j][...]
+
+            for j in range(4):
+                rows = span(ids_ref[0] ^ j, size)
+                x = x_ref[rows, :]
+                _, _, gate = attend(x, x, down_ref[0], up_ref[0])
+                u = (gate * x.astype(F32)).astype(BF)
+                fields[j][0] = u
+                value = fold_taps(dot(u, w_ref[0]), cols)
+                feats[j][0] = value.astype(BF)
+                kept = value * mask_ref[rows, :].astype(F32)
+                cells[0, span(ids_ref[0] ^ j, size // 4), :] = pool_pairs(
+                    kept, pairs_ref, cols
+                ).astype(BF)
+
+        @pl.when(ids_ref[2] == 1)
+        def _():
+            for j in range(4):
+                device = ids_ref[0] ^ j
+                before = jnp.where(t > 0, label_at(label_ref, ids_ref, device, 0), 0)
+                before += jnp.where(t > 1, label_at(label_ref, ids_ref, device, 1), 0)
+
+                @pl.when(t == 0)
+                def _(j=j):
+                    du[j][...] = jnp.zeros_like(du[j])
+
+                @pl.when(label_at(label_ref, ids_ref, device, t) == 1)
+                def _(j=j, before=before):
+                    taps = spread_taps(cot_in[j][0].astype(F32), cols)
+                    du[j][before] = dot_nt(taps, w_ref[0]).astype(BF)
+
+    def step(shape, only=None):
+        return pl.BlockSpec(
+            (1,) + shape[1:],
+            lambda t, ids, _: (t if only is None else jnp.where(ids[2] == only, t, 0),)
+            + (0,) * (len(shape) - 1),
+        )
+
+    def same(shape):
+        return pl.BlockSpec(shape, lambda t, ids, _: (0,) * len(shape))
+
+    outs = [(tasks_n, size, channels)] * 4 + [(tasks_n, size, LANES)] * 5 + [(2, size, channels)] * 4
+    args = list(x_slices) + [down, up_t, weights, mask] + list(cots)
+    results = pl.pallas_call(
+        unread(body, 1, 2 + len(args)),
+        grid_spec=pltpu.PrefetchScalarGridSpec(
+            num_scalar_prefetch=2,
+            grid=(tasks_n,),
+            in_specs=[same(a.shape) for a in x_slices]
+            + [step(down.shape, 0), step(up_t.shape, 0), step(weights.shape), same(mask.shape)]
+            + [step(a.shape, 1) for a in cots]
+            + [pl.BlockSpec(memory_space=pl.ANY)],
+            out_specs=[step(shape, 0) for shape in outs[:9]] + [same(shape) for shape in outs[9:]],
+            scratch_shapes=[pltpu.VMEM((pixels, channels), BF), pltpu.VMEM((size // 2, LANES), F32)],
+        ),
+        out_shape=[jax.ShapeDtypeStruct(shape, BF) for shape in outs],
+        compiler_params=pltpu.CompilerParams(vmem_limit_bytes=VMEM_BYTES),
+        cost_estimate=LIGHT,
+        name="section_tasks",
+    )(line.ids, labels, *args, line.last)
+    line.last = results[-1]
+    return results[:4], results[4:8], results[8], results[9:]
+
+
+def grads_of_taps(field, grad_at, taps_ref, flat, out_at, cols, depth):
+    size = taps_ref.shape[0] // 4
+    for i in range(4 if grad_at is not None else 0):
+        taps_ref[i * size : (i + 1) * size, :] = spread_taps(grad_at(i).astype(F32), cols)
+    channels = field.shape[1]
+    for row in range(3):
+        whole = dot_tn(field, taps_ref[:, row * 3 * LANES : (row + 1) * 3 * LANES])
+        for b in range(3):
+            tap = 3 * row + b
+            flat[tap * channels : (tap + 1) * channels, :] = whole[
+                :, b * LANES : (b + 1) * LANES
+            ].astype(BF)
+    for r in range(4):
+        out = out_at(r)
+        for p in range(4):
+            chunk = p * 4 + r
+            out[p] = flat[chunk * depth : (chunk + 1) * depth, :]
+
+
+def trunk_grads(line, enc_pairs, dec_pairs, depth, cols, name):
+    count = len(enc_pairs)
+    pixels, channels = enc_pairs[0][0].shape
+    size = pixels // 4
+    enc_in = [a for pair in enc_pairs for a in pair]
+    dec_in = [a for pair in dec_pairs for a in pair]
+
+    def body(ids_ref, *refs):
+        given, out, taps_ref, flat = refs[: 2 * count], *refs[2 * count :]
+        for n in range(count):
+            h_ref, g_ref = given[2 * n], given[2 * n + 1]
+            grads_of_taps(
+                h_ref[...],
+                lambda i: g_ref[i * size : (i + 1) * size, :],
+                taps_ref,
+                flat,
+                lambda r: out.at[r, n],
+                cols,
+                depth,
+            )
+
+    return section_call(
+        body,
+        [((4, count, 4, depth, LANES), BF)],
+        line,
+        enc_in,
+        name,
+        scratch=[
+            pltpu.VMEM((pixels, TAPS * LANES), BF),
+            pltpu.VMEM((TAPS * channels, LANES), BF),
+        ],
+        paired=enumerate(dec_in),
+    )[0]
+
+
+def dec_task_grads(line, dec_xs, q_cells, mask, att, cots, depth, cols):
+    tasks_n, size, _ = q_cells[0].shape
+    pixels, channels = 4 * size, att.shape[1]
+
+    def body(ids_ref, *refs, parts):
+        x_in, q_in, mask_ref, att_ref, cot_in = refs[:4], refs[4:8], refs[8], refs[9], refs[10:14]
+        u_ref, out, taps_ref, flat, x_ref, s_ref, pairs_ref = refs[14:]
+        for j in range(4):
+            x_ref[:, span(ids_ref[0] ^ j, LANES)] = x_in[j][...]
+        for t in range(tasks_n):
+            for i in range(4):
+                image = ids_ref[0] ^ i
+                rows = span(image, size)
+                x_low = x_ref[rows, :]
+                x = x_low.astype(F32)
+                own = mask_ref[rows, :]
+                for j in range(4):
+                    kept = q_in[j][t, span(image, size // 4), :].astype(F32)
+                    cells = spread_pairs(kept, pairs_ref, cols)
+                    s_ref[:, span(ids_ref[0] ^ j, LANES)] = cells.astype(BF) * own
+                mixture = (x + s_ref[...].astype(F32)).astype(BF)
+                _, _, gate = attend(x_low, mixture, att_ref[t], att_ref[tasks_n + t])
+                u_ref[t, i * size : (i + 1) * size, :] = (gate * x).astype(BF)
+            parts.send(0, t)
+            grads_of_taps(
+                u_ref[t],
+                lambda i: cot_in[i][t],
+                taps_ref,
+                flat,
+                lambda r: out.at[r, t],
+                cols,
+                depth,
+            )
+
+    return section_call(
+        body,
+        [((tasks_n, pixels, channels), BF), ((4, tasks_n, 4, depth, LANES), BF)],
+        line,
+        list(dec_xs) + list(q_cells) + [mask, att] + list(cots),
+        "dec_task_grads",
+        scratch=[
+            pltpu.VMEM((pixels, TAPS * LANES), BF),
+            pltpu.VMEM((TAPS * channels, LANES), BF),
+            pltpu.VMEM((pixels, channels), BF),
+            pltpu.VMEM((size, channels), BF),
+            pltpu.VMEM((size // 2, LANES), F32),
+        ],
+        only=1,
+        split_out=(0,),
+    )
+
+
+def enc_tasks_reverse(line, labels, grad_pieces, fields, weights, mask, dec_grads, depth, cols):
+    tasks_n, given_size, _ = grad_pieces[0].shape
+    channels = weights.shape[1]
+    size = 4 * given_size
+    pixels = 4 * size
+
+    def body(ids_ref, label_ref, *refs, parts):
+        given, u_in, w_ref, mask_ref, outs = refs[:4], refs[4:8], refs[8], refs[9], refs[10:14]
+        grads, pairs_ref, taps_ref, flat, whole = refs[14:]
+        for j in range(4):
+            outs[j][1] = jnp.zeros((size, channels), BF)
+        for t in range(tasks_n):
+            parts.need(8, t)
+            for j in range(4):
+                rows = slice(j * size, (j + 1) * size)
+                cells = spread_pairs(given[j][t].astype(F32), pairs_ref, cols)
+                grad = cells.astype(BF) * mask_ref[span(ids_ref[0] ^ j, size), :]
+                taps_ref[rows, :] = spread_taps(grad.astype(F32), cols)
+                device = ids_ref[0] ^ j
+
+                @pl.when(label_at(label_ref, ids_ref, device, t) == 1)
+                def _(t=t, j=j, rows=rows, device=device):
+                    slot = slot_of(label_ref, ids_ref, device, t)
+                    outs[j][slot] = dot_nt(taps_ref[rows, :], w_ref[t]).astype(BF)
+
+                parts.need(4 + j, t)
+                whole[rows, :] = u_in[j][t]
+            grads_of_taps(whole[...], None, taps_ref, flat, lambda r: grads.at[r, t], cols, depth)
+
+    return section_call(
+        body,
+        [((2, size, channels), BF)] * 4 + [((4, tasks_n, 4, depth, LANES), BF)],
+        line,
+        list(grad_pieces) + list(fields) + [weights, mask],
+        "enc_tasks_back",
+        scratch=[
+            pltpu.VMEM((size // 2, LANES), F32),
+            pltpu.VMEM((pixels, TAPS * LANES), BF),
+            pltpu.VMEM((TAPS * channels, LANES), BF),
+            pltpu.VMEM((pixels, channels), BF),
+        ],
+        only=0,
+        other={4: dec_grads},
+        split_in=range(4, 9),
+        smem=[labels],
+    )
+
+
+def dec_task_layer(line, fields, weights, enc_feats, cols, name):
+    tasks_n, channels, _ = weights.shape
+    size = fields.shape[1] // 4
+
+    def body(ids_ref, u_ref, w_ref, *outs, parts):
+        for t in range(tasks_n):
+            parts.need(1, t)
+            parts.need(0, t)
+            for j in range(4):
+                value = dot(u_ref[t, j * size : (j + 1) * size, :], w_ref[t])
+                outs[j][t] = fold_taps(value, cols).astype(BF)
+
+    return section_call(
+        body,
+        [((tasks_n, size, LANES), BF)] * 4,
+        line,
+        [fields, weights],
+        name,
+        only=1,
+        other=enumerate(enc_feats),
+        split_in=(0, 1),
+    )
+
+
+def heads_reverse(line, labels, x_pieces, carried, mask, du_pieces, att, cols, name, only, other=None):
+    size = x_pieces[0].shape[0] // 4
+    channels = att.shape[1]
+    tasks_n = att.shape[0] // 2
+    carry = carried is not None
+
+    def body(ids_ref, label_ref, *refs):
+        x_in, rest = refs[:4], refs[4:]
+        if carry:
+            q_in, mask_ref, rest = rest[:4], rest[4], rest[5:]
+        du_in, att_ref, rest = rest[:4], rest[4], rest[5:]
+        outs, (x_ref, s_ref, ds_ref, da_ref, pairs_ref) = rest[:-5], rest[-5:]
+        dx_ref, g_ref, grads = outs[0], outs[1], outs[2:6]
+        for j in range(4):
+            x_ref[:, span(ids_ref[0] ^ j, LANES)] = x_in[j][span(ids_ref[0], size), :]
+
+        def task(t):
+            x_low = x_ref[...]
+            x = x_low.astype(F32)
+            slot = slot_of(label_ref, ids_ref, ids_ref[0], t)
+            if carry:
+                own = mask_ref[span(ids_ref[0], size), :]
+                for j in range(4):
+                    kept = q_in[j][t, span(ids_ref[0], size // 4), :].astype(F32)
+                    cells = spread_pairs(kept, pairs_ref, cols)
+                    s_ref[:, span(ids_ref[0] ^ j, LANES)] = cells.astype(BF) * own
+                mixture = (x + s_ref[...].astype(F32)).astype(BF)
+            else:
+                mixture = x_low
+            inner, active, gate = attend(x, mixture, att_ref[t], att_ref[tasks_n + t])
+            du = (
+                (du_in[0][slot].astype(F32) + du_in[1][slot].astype(F32))
+                + (du_in[2][slot].astype(F32) + du_in[3][slot].astype(F32))
+            )
+            gated = du * gate
+            do = (gated * x * (1.0 - gate)).astype(BF)
+            sig = jax.nn.sigmoid(inner)
+            dk = (dot(do, att_ref[tasks_n + t]) * (sig * (1.0 + inner * (1.0 - sig)))).astype(BF)
+            ds = dot_nt(dk, att_ref[t])
+            dx_ref[t] = gated + ds
+            if carry:
+                ds_ref[...] = ds
+                for j in range(4):
+                    kept = ds_ref[:, span(ids_ref[0] ^ j, LANES)] * own.astype(F32)
+                    outs[6 + j][t] = pool_pairs(kept, pairs_ref, cols).astype(BF)
+            for row, value in ((t, dot_tn(mixture, dk)), (tasks_n + t, dot_tn(do, active))):
+                da_ref[...] = value
+                for j in range(4):
+                    grads[j][row] = da_ref[span(ids_ref[0] ^ j, LANES), :].astype(BF)
+
+        def no_task(t):
+            dx_ref[t] = jnp.zeros((size, channels), F32)
+            for j in range(4):
+                if carry:
+                    outs[6 + j][t] = jnp.zeros((size // 4, LANES), BF)
+                grads[j][t] = jnp.zeros((LANES, LANES), BF)
+                grads[j][tasks_n + t] = jnp.zeros((LANES, LANES), BF)
+
+        for t in range(tasks_n):
+            label = label_at(label_ref, ids_ref, ids_ref[0], t)
+            pl.when(label == 1)(functools.partial(task, t))
+            pl.when(label != 1)(functools.partial(no_task, t))
+        row = 0
+        g_ref[...] = jnp.zeros_like(g_ref)
+        for a in range(tasks_n):
+            for b in range(a, tasks_n):
+                line_sum = jnp.sum(dx_ref[a] * dx_ref[b], axis=0, keepdims=True)
+                folded = line_sum[:, :LANES]
+                for part in range(1, channels // LANES):
+                    folded = folded + line_sum[:, part * LANES : (part + 1) * LANES]
+                g_ref[row : row + 1, :] = folded
+                row += 1
+
+    outs = [((tasks_n, size, channels), F32), ((8, LANES), F32)]
+    outs += [((2 * tasks_n, LANES, LANES), BF)] * 4
+    if carry:
+        outs += [((tasks_n, size // 4, LANES), BF)] * 4
+    return section_call(
+        body,
+        outs,
+        line,
+        list(x_pieces) + (list(carried) + [mask] if carry else []) + list(du_pieces) + [att],
+        name,
+        scratch=[
+            pltpu.VMEM((size, channels), BF),
+            pltpu.VMEM((size, channels), BF),
+            pltpu.VMEM((size, channels), F32),
+            pltpu.VMEM((channels, LANES), F32),
+            pltpu.VMEM((size // 2, LANES), F32),
+        ],
+        only=only,
+        other=other,
+        smem=[labels],
+    )
+
+
+def nash_values(lines, tasks_n):
+    def full(row):
+        return jnp.broadcast_to(jnp.sum(lines[row : row + 1, :], axis=1, keepdims=True), (8, LANES))
+
+    gram = [[None] * tasks_n for _ in range(tasks_n)]
+    row = 0
+    for a in range(tasks_n):
+        for b in range(a, tasks_n):
+            gram[a][b] = gram[b][a] = full(row)
+            row += 1
+    trace_mean = (gram[0][0] + gram[1][1] + gram[2][2]) / 3.0 + 1e-06
+    norm = [[gram[a][b] / trace_mean for b in range(3)] for a in range(3)]
+    alpha = [lax.rsqrt(norm[a][a] + 1e-06) for a in range(3)]
+    for _ in range(NASH_ITERS):
+        right = [
+            norm[a][0] * alpha[0] + norm[a][1] * alpha[1] + norm[a][2] * alpha[2] - 1.0 / alpha[a]
+            for a in range(3)
+        ]
+        matrix = [
+            [norm[a][b] + 1.0 / (alpha[a] * alpha[a]) if a == b else norm[a][b] for b in range(3)]
+            for a in range(3)
+        ]
+        cof = [[None] * 3 for _ in range(3)]
+        for a in range(3):
+            for b in range(3):
+                a1, a2, b1, b2 = (a + 1) % 3, (a + 2) % 3, (b + 1) % 3, (b + 2) % 3
+                cof[a][b] = matrix[a1][b1] * matrix[a2][b2] - matrix[a1][b2] * matrix[a2][b1]
+        determinant = (
+            matrix[0][0] * cof[0][0] + matrix[0][1] * cof[0][1] + matrix[0][2] * cof[0][2]
+        )
+        update = [
+            (cof[0][b] * right[0] + cof[1][b] * right[1] + cof[2][b] * right[2]) / determinant
+            for b in range(3)
+        ]
+        alpha = [alpha[a] * jnp.exp(-0.5 * jnp.tanh(update[a] / alpha[a])) for a in range(3)]
+    return alpha
+
+
+def weigh(line, dx, w_or_lines, solve, name):
+    tasks_n, size, channels = dx.shape
+
+    def body(ids_ref, *refs):
+        given, dx_ref, outs, total = refs[: len(w_or_lines)], refs[len(w_or_lines)], refs[-6:-1], refs[-1]
+        if solve:
+            lines = (given[0][0] + given[0][1]) + (given[0][2] + given[0][3])
+            alpha = nash_values(lines, tasks_n)
+            outs[0][...] = jnp.concatenate(
+                [alpha[t][:1] for t in range(3)] + [jnp.zeros((5, LANES), F32)], axis=0
+            )
+        else:
+            outs[0][...] = given[0][...]
+        acc = None
+        for t in range(tasks_n):
+            scale = jnp.tile(outs[0][t : t + 1, :], (1, channels // LANES))
+            term = dx_ref[t] * scale
+            acc = term if acc is None else acc + term
+        total[...] = acc
+        for j in range(4):
+            outs[1 + j][...] = total[:, span(ids_ref[0] ^ j, LANES)].astype(BF)
+
+    return kernel_call(
+        body,
+        [((8, LANES), F32)] + [((size, LANES), BF)] * 4,
+        line,
+        list(w_or_lines) + [dx],
+        name,
+        scratch=[pltpu.VMEM((size, channels), F32)],
+    )
+
+
+def trunk_reverse(
+    line, pieces, by_image, cells, mask, normed, inverse, norms, layer, weight, cols, parts, other, name, only
+):
+    pixels = normed.shape[0]
+    size = pixels // 4
+    channels = weight.shape[1]
+    takes, gives = cells is not None, "cells" in parts
+    shapes = {"slices": (pixels, LANES), "images": (size, channels), "cells": (size, LANES)}
+
+    def body(ids_ref, *refs):
+        given, rest = refs[:4], refs[4:]
+        if takes:
+            cells_in, rest = rest[:4], rest[4:]
+        if takes or gives:
+            mask_ref, rest = rest[0], rest[1:]
+        (n_ref, inv_ref, norm_ref, w_ref), rest = rest[:4], rest[4:]
+        if other is not None:
+            other_in, rest = rest[:4], rest[4:]
+        outs, (acc_ref, back_ref, pairs_ref) = rest[:-3], rest[-3:]
+        gain = norm_ref[layer : layer + 1, :]
+
+        @pl.when(ids_ref[2] == only)
+        def _():
+            if by_image:
+                for j in range(4):
+                    acc_ref[span(ids_ref[0] ^ j, size), :] = given[j][...].astype(F32)
+            else:
+                acc_ref[...] = (given[0][...].astype(F32) + given[1][...].astype(F32)) + (
+                    given[2][...].astype(F32) + given[3][...].astype(F32)
+                )
+            grad = acc_ref[...]
+            if takes:
+                start = (cells_in[0][...].astype(F32) + cells_in[1][...].astype(F32)) + (
+                    cells_in[2][...].astype(F32) + cells_in[3][...].astype(F32)
+                )
+                start = start.astype(BF).astype(F32)
+                grad = grad + spread_pairs(start, pairs_ref, cols) * mask_ref[...].astype(F32)
+            normed_value = n_ref[...]
+            preact = gain * normed_value + norm_ref[2 + layer : 3 + layer, :]
+            sig = jax.nn.sigmoid(preact)
+            dp = grad * (sig * (1.0 + preact * (1.0 - sig)))
+            bias_total = jnp.sum(dp, axis=0, keepdims=True)
+            gain_total = jnp.sum(dp * normed_value, axis=0, keepdims=True)
+            outs[1][...] = jnp.concatenate(
+                [gain_total, bias_total, jnp.zeros((6, LANES), F32)], axis=0
+            )
+            scale = inv_ref[0:1, :] * gain
+            dv = scale * (dp - bias_total / pixels - normed_value * (gain_total / pixels))
+            outs[0][...] = dv.astype(BF)
+            acc_ref[...] = dv.astype(BF).astype(F32)
+            for i in range(4):
+                part = slice(i * size, (i + 1) * size)
+                back_ref[part, :] = dot_nt(spread_taps(acc_ref[part, :], cols), w_ref[0])
+            for at, kind in enumerate(parts):
+                for j in range(4):
+                    peer = ids_ref[0] ^ j
+                    out = outs[2 + 4 * at + j]
+                    if kind == "images":
+                        out[...] = back_ref[span(peer, size), :].astype(BF)
+                    elif kind == "slices":
+                        out[...] = back_ref[:, span(peer, LANES)].astype(BF)
+                    else:
+                        kept = back_ref[:, span(peer, LANES)] * mask_ref[...].astype(F32)
+                        out[...] = pool_pairs(kept, pairs_ref, cols).astype(BF)
+
+        if other is not None:
+
+            @pl.when(ids_ref[2] != only)
+            def _():
+                for j in range(4):
+                    outs[2 + 4 * parts.index("images") + j][...] = other_in[j][...]
+
+    outs = [((pixels, LANES), BF), ((8, LANES), F32)]
+    for kind in parts:
+        outs += [(shapes[kind], BF)] * 4
+    extra = list(cells) if takes else []
+    if takes or gives:
+        extra.append(mask)
+    return kernel_call(
+        body,
+        outs,
+        line,
+        list(pieces) + extra + [normed, inverse, norms, weight] + list(other or []),
+        name,
+        scratch=[
+            pltpu.VMEM((pixels, LANES), F32),
+            pltpu.VMEM((pixels, channels), F32),
+            pltpu.VMEM((pixels // 2, LANES), F32),
+        ],
+    )
+
+
+def plane_device(
+    x_in,
+    pool_index,
+    task_mask,
+    task_cot,
+    trunk_conv,
+    norm_gain,
+    norm_bias,
+    att_down,
+    attention_up_weights,
+    task_conv,
+):
+    micro_count, _, rows_n, cols, channels = x_in.shape
+    tasks_n = task_cot.shape[0]
+    strip = rows_n * cols
+    size = strip * micro_count
+    depth = trunk_conv.shape[2]
+    part = att_down.shape[2]
+    section = lax.axis_index("pipe")
+    decoder = section == 1
+    row_at = lax.axis_index("rows")
+    line = Line(jnp.stack([lax.axis_index("dp"), row_at, section]).astype(jnp.int32))
+    ENC, DEC, BOTH = (0,), (1,), (0, 1)
+
+    norm_own = jnp.concatenate([norm_gain[0], norm_bias[0]], axis=0)
+    own_lanes = jnp.arange(LANES) // part == row_at
+    norm_own = jnp.where(own_lanes[None], jnp.tile(norm_own, (1, LANES // part)), 0).astype(BF)
+    norm_own = jnp.pad(norm_own, ((0, 12), (0, 0)))
+    att_own = jnp.concatenate(
+        [att_down[0], jnp.swapaxes(attention_up_weights[0], 1, 2)], axis=0
+    ).reshape(2 * tasks_n * part, LANES)
+
+    trunk_cut = trade(cut_weights(line, [(trunk_conv[0], [0, 1])], "cut_trunk"), "dp", BOTH)
+
+    labels = lax.all_gather(task_mask, "dp").reshape(-1)
+
+    picked = pool_index[:, 0, :, None, :, None]
+    place = jnp.arange(2)[:, None, None] * 2 + jnp.arange(2)[None, None, :]
+    cells = (picked == place[None, None]).astype(BF)
+    cells = jnp.broadcast_to(cells.reshape(micro_count, strip, 1), (micro_count, strip, LANES))
+    strips = x_in.reshape(micro_count, strip, channels)
+
+    def cut_input(ids_ref, x_ref, m_ref, *outs):
+        for j in range(4):
+            outs[j][:, :channels] = x_ref[ids_ref[1] ^ j]
+            outs[j][:, channels:] = m_ref[ids_ref[1] ^ j]
+
+    strips = kernel_call(
+        cut_input, [((strip, channels + LANES), BF)] * 4, line, [strips, cells], "cut_input"
+    )
+    strips = trade(strips, "rows", BOTH)
+
+    trunk_block = stack_weights(line, trunk_cut, [[0, 1]], [[norm_own, att_own]], "stack_trunk")[0]
+    trunk_all = lax.all_gather(trunk_block, "rows")
+
+    def place_input(ids_ref, a, b, c, e, o_ref):
+        for j, piece in enumerate((a, b, c, e)):
+            o_ref[span(ids_ref[1] ^ j, strip), :] = piece[...]
+
+    x_image = kernel_call(
+        place_input, [((size, channels + LANES), BF)], line, strips, "place_input"
+    )[0]
+    x_images = trade([x_image] * 4, "dp", ENC)
+    task_cut = trade(
+        cut_weights(line, [(task_conv[0], range(tasks_n))], "cut_tasks"), "dp", BOTH
+    )
+    anchor(line, x_images, "input_there")
+    task_block = stack_weights(line, task_cut, [list(range(tasks_n))], [[]], "stack_tasks")[0]
+    task_all = lax.all_gather(task_block, "rows")
+
+    half = channels // 2
+
+    def cut_cot(ids_ref, mask_ref, c_ref, *outs):
+        for j in range(4):
+            micro = ids_ref[1] ^ j
+            for t in range(tasks_n):
+                labelled = mask_ref[micro * tasks_n + t].astype(F32)
+                value = c_ref[t, micro, :, span(ids_ref[2], half)].astype(F32)
+                outs[j][t] = (value * labelled).astype(BF)
+
+    cot_strips = kernel_call(
+        cut_cot,
+        [((tasks_n, strip, half), BF)] * 4,
+        line,
+        [task_cot.reshape(tasks_n, micro_count, strip, channels)],
+        "cut_cotangents",
+        smem=[task_mask.reshape(-1)],
+    )
+    cot_strips = trade(cot_strips, "rows", BOTH)
+
+    def place_cot(ids_ref, _, a, b, c, e, o_ref):
+        for j, piece in enumerate((a, b, c, e)):
+            for t in range(tasks_n):
+                o_ref[t, span(ids_ref[1] ^ j, strip), :] = piece[t]
+
+    cot_half = kernel_call(
+        place_cot, [((tasks_n, size, half), BF)], line, cot_strips, "place_cotangents", smem=[labels]
+    )[0]
+    cot_other = swap_sections([cot_half])[0]
+
+    def slice_cot(ids_ref, own_ref, other_ref, *rest):
+        outs, image = rest[:4], rest[4]
+        image[:, :, :half] = other_ref[...]
+        image[:, :, half:] = own_ref[...]
+        for j in range(4):
+            outs[j][...] = image[:, :, span(ids_ref[0] ^ j, LANES)]
+
+    cots = kernel_call(
+        slice_cot,
+        [((tasks_n, size, LANES), BF)] * 4,
+        line,
+        [cot_half, cot_other],
+        "slice_cotangents",
+        scratch=[pltpu.VMEM((tasks_n, size, channels), BF)],
+    )
+    cots = trade(cots, "dp", BOTH)
+    first_w, second_w, norms, att_rows = place_weights(
+        line, trunk_all, 2, depth, "place_trunk", norm_own.shape[0], att_own.shape[0]
+    )
+    enc_h0, enc_n1, enc_i1, enc_h, mask = trunk_layer(
+        line, x_images, first_w, norms, 0, cols, eps, "images", False, None, "enc_layer1", 0
+    )
+    enc_hs = trade([enc_h] * 4, "dp", ENC)
+    dec_mask = swap_sections([mask])[0]
+    att = place_attention(line, trade([att_rows] * 4, "dp", BOTH), 2 * tasks_n, part)
+    enc_h1, enc_n2, enc_i2, enc_x, z = trunk_layer(
+        line, enc_hs, second_w, norms, 1, cols, eps, "slices", True, mask, "enc_layer2", 0
+    )
+    z_pieces = swap_sections([z] * 4)
+    enc_xs = trade([enc_x] * 4, "dp", ENC)
+
+    dec_h0, dec_n1, dec_i1, dec_h = trunk_layer(
+        line, z_pieces, first_w, norms, 0, cols, eps, "cells", False, dec_mask, "dec_layer1", 1
+    )
+    dec_hs = trade([dec_h] * 4, "dp", DEC)
+
+    dec_h1, dec_n2, dec_i2, dec_x = trunk_layer(
+        line, dec_hs, second_w, norms, 1, cols, eps, "slices", True, None, "dec_layer2", 1
+    )
+    dec_xs = trade([dec_x] * 4, "dp", BOTH)
+
+    task_w = place_weights(line, task_all, tasks_n, depth, "place_tasks")[0]
+    enc_us, enc_feats, kept, du = section_tasks(
+        line, labels, enc_xs, att, task_w, mask, cots, cols
+    )
+    anchor(line, dec_xs, "decoder_there")
+    dec_du = trade(du, "dp", DEC)
+    q_cells = swap_sections([kept] * 4)
+
+    dec_dx, lines, *rest = heads_reverse(
+        line, labels, dec_xs, q_cells, dec_mask, dec_du, att, cols, "dec_heads", 1
+    )
+    dec_att, ds = rest[:4], rest[4:]
+    ds = swap_sections(ds)
+    lines = jnp.sum(lax.all_gather(lines, "dp"), axis=0)
+    terms = lax.all_gather(lines, "rows")
+    dec_w, *dh = weigh(line, dec_dx, [terms], True, "bargain")
+    dh = trade(dh, "dp", BOTH)
+    enc_w = swap_sections([dec_w])[0]
+    nash_w = jnp.where(decoder, dec_w, enc_w)
+
+    dec_dv2, dec_s2, *dh = trunk_reverse(
+        line, dh, True, None, None, dec_n2, dec_i2, norms, 1, second_w, cols, ["slices"], None, "dec_back2", 1
+    )
+    dh = trade(dh, "dp", DEC)
+    dec_u, dec_dw = dec_task_grads(line, dec_xs, q_cells, dec_mask, att, cots, depth, cols)
+    dec_dv1, dec_s1, *rest = trunk_reverse(
+        line, dh, False, None, dec_mask, dec_n1, dec_i1, norms, 0, first_w, cols, ["cells", "images"], None, "dec_back1", 1
+    )
+    dec_start, dec_dz = swap_sections(rest[:4]), rest[4:]
+    *du, task_dw = enc_tasks_reverse(
+        line, labels, ds, enc_us, task_w, mask, dec_dw, depth, cols
+    )
+    enc_du = trade(du, "dp", ENC)
+    task_dw = lax.psum_scatter(task_dw, "rows", scatter_dimension=0, tiled=True)
+    enc_dx, _, *att_parts = heads_reverse(
+        line, labels, enc_xs, None, None, enc_du, att, cols, "enc_heads_back", 0, {k + 2: a for k, a in enumerate(dec_att)}
+    )
+    _, *dh = weigh(line, enc_dx, [enc_w], False, "enc_weigh")
+    dh = trade(dh, "dp", BOTH)
+    att_parts = trade(att_parts, "dp", BOTH)
+
+    feats = dec_task_layer(line, dec_u, task_w, enc_feats, cols, "dec_tasks")
+    feats = trade(feats, "dp", BOTH)
+    enc_dv2, enc_s2, *dh = trunk_reverse(
+        line, dh, True, dec_start, mask, enc_n2, enc_i2, norms, 1, second_w, cols, ["slices"], None, "enc_back2", 0
+    )
+    dh = trade(dh, "dp", ENC)
+
+    enc_dv1, enc_s1, *dz = trunk_reverse(
+        line, dh, False, None, None, enc_n1, enc_i1, norms, 0, first_w, cols, ["images"], dec_dz, "enc_back1", 0
+    )
+    dz = trade(dz, "dp", BOTH)
+    trunk_dw = trunk_grads(
+        line,
+        [(enc_h0, enc_dv1), (enc_h1, enc_dv2)],
+        [(dec_h0, dec_dv1), (dec_h1, dec_dv2)],
+        depth,
+        cols,
+        "trunk_grads",
+    )
+    trunk_dw = lax.psum_scatter(trunk_dw, "rows", scatter_dimension=0, tiled=True)
+
+
+    def share(sums, name):
+        counts = [a.shape[1] for a in sums]
+
+        def cut(ids_ref, *refs):
+            outs = refs[len(sums) :]
+            for j in range(4):
+                row = 0
+                for ref, count in zip(refs, counts):
+                    for n in range(count):
+                        outs[j][row] = ref[0, n, ids_ref[0] ^ j]
+                        row += 1
+
+        pieces = kernel_call(cut, [((sum(counts), depth, LANES), BF)] * 4, line, sums, name)
+        return trade(pieces, "dp", BOTH)
+
+    def join(layers, scale, name):
+        counts = [pieces[0].shape[0] for pieces in layers]
+
+        def body(ids_ref, *refs):
+            o_ref, at = refs[-1], 0
+            for m, count in enumerate(counts):
+                for n in range(count):
+                    for j in range(4):
+                        value = refs[4 * m + j][n].astype(F32)
+                        if scale is not None:
+                            value = value * refs[4 * len(counts)][n : n + 1, :]
+                        o_ref[at, :, span(ids_ref[0] ^ j, LANES)] = value
+                    at += 1
+
+        return kernel_call(
+            body,
+            [((sum(counts), depth, channels), F32)],
+            line,
+            [piece for pieces in layers for piece in pieces] + ([] if scale is None else [scale]),
+            name,
+        )[0]
+
+    def cut_att(ids_ref, a, b, c, e, *rest):
+        outs, total = rest[:4], rest[4]
+        total[...] = (a[...].astype(F32) + b[...].astype(F32)) + (
+            c[...].astype(F32) + e[...].astype(F32)
+        )
+        for j in range(4):
+            outs[j][...] = total[:, span(ids_ref[1] ^ j, part), :].astype(BF)
+
+    att_parts = kernel_call(
+        cut_att,
+        [((2 * tasks_n, part, LANES), BF)] * 4,
+        line,
+        att_parts,
+        "cut_attention",
+        scratch=[pltpu.VMEM((2 * tasks_n, LANES, LANES), F32)],
+    )
+    att_parts = trade(att_parts, "rows", BOTH)
+
+    def cut_feats(ids_ref, a, b, c, e, *rest):
+        outs, image = rest[:4], rest[4]
+        for j, piece in enumerate((a, b, c, e)):
+            image[:, :, span(ids_ref[0] ^ j, LANES)] = piece[...]
+        for j in range(4):
+            outs[j][...] = image[:, span(ids_ref[1] ^ j, strip), :]
+
+    feats = kernel_call(
+        cut_feats,
+        [((tasks_n, strip, channels), BF)] * 4,
+        line,
+        feats,
+        "cut_features",
+        scratch=[pltpu.VMEM((tasks_n, size, channels), BF)],
+    )
+    feats = trade(feats, "rows", BOTH)
+
+    sums = jnp.where(
+        decoder, jnp.concatenate([dec_s1, dec_s2]), jnp.concatenate([enc_s1, enc_s2])
+    )
+    sums = trade([sums] * 4, "rows", BOTH)
+    sums = (sums[0] + sums[1]) + (sums[2] + sums[3])
+    sums = lax.dynamic_slice_in_dim(sums, row_at * part, part, axis=1)
+    gain_out = jnp.stack([sums[0], sums[8]])
+    bias_out = jnp.stack([sums[1], sums[9]])
+
+    def cut_start(ids_ref, a, b, c, e, *rest):
+        outs, image = rest[:4], rest[4]
+        image[...] = (a[...].astype(F32) + b[...].astype(F32)) + (
+            c[...].astype(F32) + e[...].astype(F32)
+        )
+        for j in range(4):
+            outs[j][...] = image[span(ids_ref[1] ^ j, strip), :].astype(BF)
+
+    starts = kernel_call(
+        cut_start,
+        [((strip, channels), BF)] * 4,
+        line,
+        dz,
+        "cut_start",
+        scratch=[pltpu.VMEM((size, channels), F32)],
+    )
+    starts = trade(starts, "rows", BOTH)
+
+    task_parts = share([task_dw], "share_tasks")
+    trunk_parts = share([trunk_dw], "share_trunk")
+
+    def place_feats(ids_ref, a, b, c, e, o_ref):
+        for j, piece in enumerate((a, b, c, e)):
+            for t in range(tasks_n):
+                o_ref[t, ids_ref[1] ^ j] = piece[t]
+
+    feats_out = kernel_call(
+        place_feats, [((tasks_n, micro_count, strip, channels), BF)], line, feats, "place_features"
+    )[0]
+
+    def join_att(ids_ref, a, b, c, e, w_ref, o_ref):
+        total = (a[...].astype(F32) + b[...].astype(F32)) + (
+            c[...].astype(F32) + e[...].astype(F32)
+        )
+        for t in range(2 * tasks_n):
+            at = t % tasks_n
+            o_ref[t] = total[t] * w_ref[at : at + 1, :]
+
+    att_out = kernel_call(
+        join_att,
+        [((2 * tasks_n, part, LANES), F32)],
+        line,
+        att_parts + [nash_w],
+        "join_attention",
+    )[0]
+
+    def place_start(ids_ref, a, b, c, e, o_ref):
+        for j, piece in enumerate((a, b, c, e)):
+            o_ref[ids_ref[1] ^ j] = piece[...].astype(F32)
+
+    start_out = kernel_call(
+        place_start, [((micro_count, strip, channels), F32)], line, starts, "place_start"
+    )[0]
+    task_out = join([task_parts], nash_w, "join_tasks")
+    trunk_out = join([trunk_parts], None, "join_trunk")
+
+    return (
+        feats_out.reshape(1, tasks_n, micro_count, 1, rows_n, cols, channels),
+        start_out.reshape(1, micro_count, 1, rows_n, cols, channels),
+        trunk_out[None],
+        gain_out[None],
+        bias_out[None],
+        att_out[:tasks_n][None],
+        jnp.swapaxes(att_out[tasks_n:], 1, 2)[None],
+        task_out[None],
+        nash_w[:3, 0],
+    )
+
+
+def by_planes(x_in, task_cot):
+    peers, planes = lax.axis_size("dp"), lax.axis_size("rows")
+    micro, samples, _, _, channels = x_in.shape
+    return (
+        peers == 4
+        and planes == 4
+        and micro == planes
+        and samples == 1
+        and channels == peers * LANES
+        and task_cot.shape[0] == 3
+    )
+
+
+def section_device(*arrays):
+    if by_planes(arrays[0], arrays[3]):
+        return plane_device(*arrays)
+    return on_device(*arrays)
+
+
 def solution(mesh):
     in_specs = (
         P(None, "dp", "rows", None, None),
@@ -457,5 +1822,5 @@
         P(),
     )
     return jax.shard_map(
-        on_device, mesh=mesh, in_specs=in_specs, out_specs=out_specs, check_vma=False
-    )
+        section_device, mesh=mesh, in_specs=in_specs, out_specs=out_specs, check_vma=False
+    )

time: 3200 us -> 476 us (0.15)
  blocking collectives: 1370 us -> 33.6 us
  waiting for transfers between devices: 792 us -> 103 us
  matrix products: 397 us -> 0 us
  Pallas kernels: 0 us -> 137 us
  starting transfers between devices: 286 us -> 150 us
  other arithmetic: 114 us -> 3.38 us
  between operations: 119 us -> 15.7 us
  local copies, waits for them, and re-layouts: 109 us -> 24.7 us
    psum x31 -> x0, blocking collectives: 1190 us -> none  [the longest x10 390 us: norm_moments(): lax.psum(jnp.sum(conv_out, axis=(0, 1, 2, 3)), ('dp', 'rows')) / pixel_count]
    reduce_scatter x3 -> x2, waiting for transfers between devices: 770 us -> 0.01 us  [the longest x1 0.01 us: plane_device(): task_dw = lax.psum_scatter(task_dw, 'rows', scatter_dimension=0, tiled=True)]
    dot_general x98 -> x0, matrix products: 397 us -> none  [the longest x15 150 us: conv_backward(): jnp.einsum('ksrwq,ksrwd->kqd', gather_taps(padded, rows_n, cols_n), grad_...]
    all_gather x4 -> x3, blocking collectives: 178 us -> 33.6 us  [the longest x1 18.1 us: plane_device(): terms = lax.all_gather(lines, 'rows')]
    pallas_call x0 -> x41, Pallas kernels: none -> 137 us  [the longest x32 86.6 us: kernel_call(): pl.pallas_call(unread(on_section(body, only), len(extra), first), out_sha...]
    ppermute x100 -> x97, starting transfers between devices: 286 us -> 150 us  [the longest x78 122 us: trade(): taken.append(lax.ppermute(pieces[j], ('pipe', axis), pairs))]
    ppermute x100 -> x97, waiting for transfers between devices: 20 us -> 103 us  [the longest x78 79.1 us: trade(): taken.append(lax.ppermute(pieces[j], ('pipe', axis), pairs))]
    add x3 -> x2, other arithmetic: 38 us -> 0.14 us  [the longest x1 0.07 us: plane_device(): sums = sums[0] + sums[1] + (sums[2] + sums[3])]
  transfers between devices with their start and end apart: 108 -> 101, of which waited for: 23 -> 30; matrix products, arithmetic and copies ran while one was open for 12% -> 2% of each run, Pallas kernels for 0% -> 23%
where the time goes in v1:
time: 476 us; the launch traced here: 467 us
  starting transfers between devices  150 us (32%)
  Pallas kernels  137 us (29%)
  waiting for transfers between devices  103 us (22%)
  blocking collectives  33.6 us (7%)
  local copies, waits for them, and re-layouts  24.7 us (5%)
  between operations  15.7 us (3%)
    ppermute x78, starting transfers between devices, trade(): taken.append(lax.ppermute(pieces[j], ('pipe', axis), pairs))  122 us
    pallas_call x32, Pallas kernels, kernel_call(): pl.pallas_call(unread(on_section(body, only), len(extra), first), out_sha...  86.6 us
    ppermute x78, waiting for transfers between devices, trade(): taken.append(lax.ppermute(pieces[j], ('pipe', axis), pairs))  79.1 us
    pallas_call x6, Pallas kernels, section_call(): pl.pallas_call(whole, out_shape=[jax.ShapeDtypeStruct(shape, dtype) for s...  35.3 us
    ppermute x19, starting transfers between devices, swap_sections(): lax.ppermute(pieces[j], ('pipe', 'dp'), [(p * count + i, (1 - p) * count...  27.6 us
    ppermute x19, waiting for transfers between devices, swap_sections(): lax.ppermute(pieces[j], ('pipe', 'dp'), [(p * count + i, (1 - p) * count...  23.7 us
    all_gather x1, blocking collectives, plane_device(): terms = lax.all_gather(lines, 'rows')  18.1 us
    unnamed x276, local copies, waits for them, and re-layouts  17.6 us
  transfers between devices with their start and end apart: 101, of which 30 were waited for; matrix products, arithmetic and copies ran while one was open for 2% of the time, Pallas kernels for 23%

profile of v1, /device:TPU:0, one launch (start us, length us, event | category | flops | bytes accessed | tf_op | source)
XLA Modules:
  0.0 467.4 jit_solution(13789105572525944118)
XLA Ops:
  9.9 3.9 collective-permute-start.5
  24.1 3.6 collective-permute-start.2
  28.5 2.5 collective-permute-done.2.refs_4_
  31.0 3.0 collective-permute-done.refs_2_
  36.4 3.4 collective-permute-start.6
  39.8 4.3 collective-permute-start.7
  46.0 2.2 cut_tasks.1
  51.8 4.0 collective-permute-done.7.refs_2_.refs_3_
  60.5 2.2 stack_tasks.1.refs_3_
  66.1 2.9 collective-permute-start.13
  69.9 7.8 %all-gather.1 = s32[16,1,3]{2,1,0:T(1,128)S(1)} all-gather(s32[4,1,3]{2,1,0:T(1,128)S(1)} %copy.37), channel_id=3, replica_groups=mesh['pipe'=2,'dp'=4,'rows'=4] {'dp'}, dimensions={0}, use_global_device_ids=true | all-gather | bytes 240 | tf_op jit(solution)/shard_map/all_gather | solution.py:1461
  88.0 3.5 place_trunk.1
  94.6 5.2 %enc_layer1.1 = (bf16[1024,512]{1,0:T(8,128)(2,1)}, f32[1024,128]{1,0:T(8,128)}, f32[8,128]{1,0:T(8,128)}, bf16[1024,128]{1,0:T(8,128)(2,1)}, bf16[1024,128]{1,0:T(8,128)(2,1)}) custom-call(s32[3]{0:T(128)} %pad_add_fusion.refs_0_, bf16[256,640]{1,0:T(8,128)(2,1)} %place_input.1.refs_2_.refs_0_.refs_1_, bf16[256,640]{1,0:T(8,128)(2,1)} %copy-done.5, ...), custom_call_target="tpu_custom_call" | custom-call | flops 300000000 | bytes 1 | tf_op jit(solution)/shard_map/enc_layer1/pallas_call | solution.py:477
  101.7 2.7 collective-permute-start.17
  104.3 4.6 collective-permute-start.18
  109.3 6.5 %collective-permute-done.21.refs_4_ = bf16[4,192,128]{2,1,0:T(8,128)(2,1)S(1)} collective-permute-done((bf16[4,192,128]{2,1,0:T(8,128)(2,1)S(1)}, bf16[4,192,128]{2,1,0:T(8,128)(2,1)S(1)}, u32[]{:S(2)}, u32[]{:S(2)}) %collective-permute-start.21) | collective-permute-done | bytes 196640 | tf_op jit(solution)/shard_map/ppermute | solution.py:655
  119.6 5.1 %enc_layer2.1 = (bf16[1024,512]{1,0:T(8,128)(2,1)}, f32[1024,128]{1,0:T(8,128)}, f32[8,128]{1,0:T(8,128)}, bf16[1024,128]{1,0:T(8,128)(2,1)}, bf16[256,128]{1,0:T(8,128)(2,1)}) custom-call(s32[3]{0:T(128)} %pad_add_fusion.refs_0_, bf16[1024,128]{1,0:T(8,128)(2,1)} %get-tuple-element.167.refs_1_, bf16[1024,128]{1,0:T(8,128)(2,1)} %copy-done.37, ...), custom_call_target="tpu_custom_call" | custom-call | flops 300000000 | bytes 1 | tf_op jit(solution)/shard_map/enc_layer2/pallas_call | solution.py:477
  128.9 3.0 collective-permute-done.24.refs_3_
  133.5 2.7 dec_layer1.1
  138.2 2.5 collective-permute-start.33
  144.5 3.1 collective-permute-start.34
  147.6 3.1 dec_layer2.1
  150.7 3.0 collective-permute-done.36.refs_11_.refs_12_
  153.7 2.6 collective-permute-start.35
  156.3 2.5 collective-permute-start.30
  161.4 4.6 place_tasks.1.refs_8_.refs_14_.refs_10_.refs_2_
  166.9 13.8 %section_tasks.1 = (bf16[3,256,512]{2,1,0:T(8,128)(2,1)}, bf16[3,256,512]{2,1,0:T(8,128)(2,1)}, bf16[3,256,512]{2,1,0:T(8,128)(2,1)}, bf16[3,256,512]{2,1,0:T(8,...) custom-call(s32[3]{0:T(128)} %pad_add_fusion.refs_0_, ...), custom_call_target="tpu_custom_call" | custom-call | flops 300000000 | bytes 1 | tf_op jit(solution)/shard_map/section_tasks/pallas_call | solution.py:970
  182.9 8.9 %collective-permute-start.39 = (bf16[3,256,128]{2,1,0:T(8,128)(2,1)}, bf16[3,256,128]{2,1,0:T(8,128)(2,1)S(1)}, u32[]{:S(2)}, u32[]{:S(2)}) collective-permute-start(bf16[3,256,128]{2,1,0:T(8,128)(2,1)} %get-tuple-element.177), channel_id=1, source_target_pairs={{0,16},{4,20},{8,24},{12,28},{16,0},{20,4},{24,8},{28,12},{1,17},{... | collective-permute-start | bytes 589832 | tf_op jit(solution)/shard_map/ppermute | solution.py:662
  194.3 9.3 %collective-permute-done.40.refs_7_.refs_6_ = bf16[3,256,128]{2,1,0:T(8,128)(2,1)S(1)} collective-permute-done((bf16[3,256,128]{2,1,0:T(8,128)(2,1)}, bf16[3,256,128]{2,1,0:T(8,128)(2,1)S(1)}, u32[]{:S(2)}, u32[]{:S(2)}) %collective-permute-start.40) | collective-permute-done | bytes 196640 | tf_op jit(solution)/shard_map/ppermute | solution.py:662
  206.0 5.3 %collective-permute-done.42.refs_9_.refs_8_ = bf16[3,256,128]{2,1,0:T(8,128)(2,1)S(1)} collective-permute-done((bf16[3,256,128]{2,1,0:T(8,128)(2,1)}, bf16[3,256,128]{2,1,0:T(8,128)(2,1)S(1)}, u32[]{:S(2)}, u32[]{:S(2)}) %collective-permute-start.42) | collective-permute-done | bytes 196640 | tf_op jit(solution)/shard_map/ppermute | solution.py:662
  214.0 7.6 %all-gather.3 = f32[32,128]{1,0:T(8,128)S(1)} all-gather(f32[8,128]{1,0:T(8,128)} %get-tuple-element.182), channel_id=5, replica_groups=mesh['pipe'=2,'dp'=4,'rows'=4] {'dp'}, dimensions={0}, use_global_device_ids=true | all-gather | bytes 20480 | tf_op jit(solution)/shard_map/all_gather | solution.py:1581
  221.6 18.1 %all-gather.4 = f32[32,128]{1,0:T(8,128)} all-gather(f32[8,128]{1,0:T(8,128)S(1)} %bitcast_reduce_fusion), channel_id=6, replica_groups=mesh['pipe'=2,'dp'=4,'rows'=4] {'rows'}, dimensions={0}, use_global_device_ids=true | all-gather | bytes 20480 | tf_op jit(solution)/shard_map/all_gather | solution.py:1582
  239.7 2.6 bargain.1
  250.3 2.7 dec_back2.1
  255.1 8.0 %collective-permute-start.53 = (bf16[3,64,128]{2,1,0:T(8,128)(2,1)S(1)}, bf16[3,64,128]{2,1,0:T(8,128)(2,1)S(1)}, u32[]{:S(2)}, u32[]{:S(2)}) collective-permute-start(bf16[3,64,128]{2,1,0:T(8,128)(2,1)S(1)} %copy-done.89), channel_id=1, source_target_pairs={{0,28},{4,24},{8,20},{12,16},{16,12},{20,8},{24,4},{28,0},{1,29},{... | collective-permute-start | bytes 147464 | tf_op jit(solution)/shard_map/ppermute | solution.py:662
  267.1 3.2 dec_back1.1
  271.0 15.1 %enc_tasks_back.1 = (bf16[2,256,512]{2,1,0:T(8,128)(2,1)}, bf16[2,256,512]{2,1,0:T(8,128)(2,1)}, bf16[2,256,512]{2,1,0:T(8,128)(2,1)}, bf16[2,256,512]{2,1,0:T(8,128)(2,1)}, bf16[4,3,4,288,128]{4,3,2,1,0:T(8,128)(2,1)}) custom-call(s32[3]{0:T(128)} %pad_add_fusion.refs_0_, s32[48]{0:T(128)} %reshape.111.refs_1_, bf16[3,64,128]{2,1,0:T(8,128)(2,1)} %copy-done.86, ...), custom_call_target="tpu_custom_call" | custom-call | flops 300000000 | bytes 1 | tf_op jit(solution)/shard_map/enc_tasks_back/pallas_call | solution.py:618
  287.1 2.9 collective-permute-start.57
  290.1 2.6 collective-permute-start.58
  292.7 3.7 collective-permute-start.59
  298.2 8.6 %collective-permute-done.58.refs_8_ = bf16[2,256,512]{2,1,0:T(8,128)(2,1)S(1)} collective-permute-done((bf16[2,256,512]{2,1,0:T(8,128)(2,1)S(1)}, bf16[2,256,512]{2,1,0:T(8,128)(2,1)S(1)}, u32[]{:S(2)}, u32[]{:S(2)}) %collective-permute-start.58) | collective-permute-done | bytes 524320 | tf_op jit(solution)/shard_map/ppermute | solution.py:655
  306.8 2.2 collective-permute-start.72
  309.0 6.8 %enc_heads_back.1 = (f32[3,256,512]{2,1,0:T(8,128)}, f32[8,128]{1,0:T(8,128)}, bf16[6,128,128]{2,1,0:T(8,128)(2,1)}, bf16[6,128,128]{2,1,0:T(8,128)(2,1)}, bf16[...) custom-call(s32[3]{0:T(128)} %pad_add_fusion.refs_0_, s32[48]{0:T(128)} %reshape.111.refs_1_, ...), custom_call_target="tpu_custom_call" | custom-call | flops 300000000 | bytes 1 | tf_op jit(solution)/shard_map/enc_heads_back/pallas_call | solution.py:618
  316.5 2.3 enc_weigh.1
  322.3 2.9 dec_tasks.1
  326.6 5.2 %enc_back2.1 = (bf16[1024,128]{1,0:T(8,128)(2,1)}, f32[8,128]{1,0:T(8,128)}, bf16[1024,128]{1,0:T(8,128)(2,1)}, bf16[1024,128]{1,0:T(8,128)(2,1)}, bf16[1024,128]{1,0:T(8,128)(2,1)}, /*index=5*/bf16[1024,128]{1,0:T(8,128)(2,1)}) custom-call(s32[3]{0:T(128)} %pad_add_fusion.refs_0_, bf16[256,128]{1,0:T(8,128)(2,1)} %get-tuple-element.232.refs_1_, ...), custom_call_target="tpu_custom_call" | custom-call | flops 300000000 | bytes 1 | tf_op jit(solution)/shard_map/enc_back2/pallas_call | solution.py:477
  331.8 2.4 collective-permute-start.73
  334.2 3.7 collective-permute-start.74
  337.9 3.1 collective-permute-start.75
  342.7 4.6 collective-permute-done.75.refs_4_
  348.1 5.3 %enc_back1.1 = (bf16[1024,128]{1,0:T(8,128)(2,1)}, f32[8,128]{1,0:T(8,128)}, bf16[256,512]{1,0:T(8,128)(2,1)}, bf16[256,512]{1,0:T(8,128)(2,1)}, bf16[256,512]{1,0:T(8,128)(2,1)}, /*index=5*/bf16[256,512]{1,0:T(8,128)(2,1)}) custom-call(s32[3]{0:T(128)} %pad_add_fusion.refs_0_, bf16[1024,128]{1,0:T(8,128)(2,1)} %get-tuple-element.241.refs_1_, ...), custom_call_target="tpu_custom_call" | custom-call | flops 300000000 | bytes 1 | tf_op jit(solution)/shard_map/enc_back1/pallas_call | solution.py:477
  353.3 8.0 %trunk_grads.1.refs_5_ = bf16[4,2,4,288,128]{4,3,2,1,0:T(8,128)(2,1)} custom-call(s32[3]{0:T(128)} %pad_add_fusion.refs_0_, bf16[1024,512]{1,0:T(8,128)(2,1)} %get-tuple-element.231.refs_1_, bf16[1024,128]{1,0:T(8,128)(2,1)} %get-tuple-element.250.refs_2_, bf16[1024,512]{1,0:T(8,128)(2,1)} %get-tuple-element.251.refs_3_, ...), custom_call_target="tpu_custom_call" | custom-call | flops 300000000 | bytes 1 | tf_op jit(solution)/shard_map/trunk_grads/pallas_call | solution.py:618
  375.8 4.3 collective-permute-done.61.refs_3_
  383.1 3.0 collective-permute-start.95
  386.2 3.9 collective-permute-start.96
  390.1 2.3 cut_features.1
  393.1 3.9 collective-permute-start.78
  402.1 14.4 %collective-permute-done.85.refs_2_ = bf16[6,32,128]{2,1,0:T(8,128)(2,1)S(1)} collective-permute-done((bf16[6,32,128]{2,1,0:T(8,128)(2,1)}, bf16[6,32,128]{2,1,0:T(8,128)(2,1)S(1)}, u32[]{:S(2)}, u32[]{:S(2)}) %collective-permute-start.85) | collective-permute-done | bytes 49184 | tf_op jit(solution)/shard_map/ppermute | solution.py:655
  417.5 13.9 %collective-permute-done.86.refs_3_ = bf16[6,32,128]{2,1,0:T(8,128)(2,1)S(1)} collective-permute-done((bf16[6,32,128]{2,1,0:T(8,128)(2,1)S(1)}, bf16[6,32,128]{2,1,0:T(8,128)(2,1)S(1)}, u32[]{:S(2)}, u32[]{:S(2)}) %collective-permute-start.86) | collective-permute-done | bytes 49184 | tf_op jit(solution)/shard_map/ppermute | solution.py:655
  435.3 2.3 collective-permute-start.83
  439.5 2.2 place_features.1.refs_6_
  441.7 2.3 collective-permute-start.93
  454.7 2.7 join_tasks.1.refs_5_
  458.2 2.3 join_trunk.1
  (492 shorter events, 140.6 us)
Async XLA Ops:
  7.2 80.8 %all-gather.8.cloned.1.call-start = ((), (), s32[]{:S(2)}) async-start(), calls=%async_computation.4 | async-start | bytes 3215360 | tf_op jit(solution)/shard_map/all_gather | solution.py:1480
  9.9 10.0 %collective-permute-start.5 = (bf16[576,128]{1,0:T(8,128)(2,1)}, bf16[576,128]{1,0:T(8,128)(2,1)S(1)}, u32[]{:S(2)}, u32[]{:S(2)}) collective-permute-start(bf16[576,128]{1,0:T(8,128)(2,1)} %get-tuple-element.147.refs_3_), channel_id=1, source_target_pairs={{0,12},{4,8},{8,4},{12,0},{16,28},{20,24},{24,20},{28,16},{1,13},{... | collective-permute-start | bytes 442376 | tf_op jit(solution)/shard_map/ppermute | solution.py:655
  24.0 137.4 %all-gather.10.cloned.1.call-start = ((), (), s32[]{:S(2)}) async-start(), calls=%async_computation.5 | async-start | bytes 4423680 | tf_op jit(solution)/shard_map/all_gather | solution.py:1495
  36.4 14.8 %collective-permute-start.6 = (bf16[256,640]{1,0:T(8,128)(2,1)}, bf16[256,640]{1,0:T(8,128)(2,1)S(1)}, u32[]{:S(2)}, u32[]{:S(2)}) collective-permute-start(bf16[256,640]{1,0:T(8,128)(2,1)} %place_input.1.refs_2_.refs_0_.refs_1_), channel_id=1, source_target_pairs={{0,4},{4,0},{8,12},{12,8},{1,5},{5,1},{9,13},{13,9},{2,6},{6,2},{1... | collective-permute-start | bytes 983048 | tf_op jit(solution)/shard_map/ppermute | solution.py:655
  39.8 16.0 %collective-permute-start.7 = (bf16[256,640]{1,0:T(8,128)(2,1)}, bf16[256,640]{1,0:T(8,128)(2,1)S(1)}, u32[]{:S(2)}, u32[]{:S(2)}) collective-permute-start(bf16[256,640]{1,0:T(8,128)(2,1)} %place_input.1.refs_2_.refs_0_.refs_1_), channel_id=1, source_target_pairs={{0,8},{4,12},{8,0},{12,4},{1,9},{5,13},{9,1},{13,5},{2,10},{6,14},... | collective-permute-start | bytes 983048 | tf_op jit(solution)/shard_map/ppermute | solution.py:655
  44.1 11.8 %collective-permute-start.8 = (bf16[256,640]{1,0:T(8,128)(2,1)}, bf16[256,640]{1,0:T(8,128)(2,1)S(1)}, u32[]{:S(2)}, u32[]{:S(2)}) collective-permute-start(bf16[256,640]{1,0:T(8,128)(2,1)} %place_input.1.refs_2_.refs_0_.refs_1_), channel_id=1, source_target_pairs={{0,12},{4,8},{8,4},{12,0},{1,13},{5,9},{9,5},{13,1},{2,14},{6,10},... | collective-permute-start | bytes 983048 | tf_op jit(solution)/shard_map/ppermute | solution.py:655
  48.3 11.4 %collective-permute-start.10 = (bf16[864,128]{1,0:T(8,128)(2,1)}, bf16[864,128]{1,0:T(8,128)(2,1)S(1)}, u32[]{:S(2)}, u32[]{:S(2)}) collective-permute-start(bf16[864,128]{1,0:T(8,128)(2,1)} %get-tuple-element.157), channel_id=1, source_target_pairs={{0,8},{4,12},{8,0},{12,4},{16,24},{20,28},{24,16},{28,20},{1,9},{5... | collective-permute-start | bytes 663560 | tf_op jit(solution)/shard_map/ppermute | solution.py:655
  62.7 337.2 %reduce-scatter.5.cloned.1.call-start = ((), (), s32[]{:S(2)}) async-start(), calls=%async_computation.3 | async-start | bytes 4423680 | tf_op jit(solution)/shard_map/reduce_scatter | solution.py:1601
  65.4 14.1 %collective-permute-start.12 = (bf16[3,64,256]{2,1,0:T(8,128)(2,1)}, bf16[3,64,256]{2,1,0:T(8,128)(2,1)S(1)}, u32[]{:S(2)}, u32[]{:S(2)}) collective-permute-start(bf16[3,64,256]{2,1,0:T(8,128)(2,1)} %get-tuple-element.160), channel_id=1, source_target_pairs={{0,1},{1,0},{2,3},{3,2},{16,17},{17,16},{18,19},{19,18},{4,5},{5,4... | collective-permute-start | bytes 294920 | tf_op jit(solution)/shard_map/ppermute | solution.py:655
  66.1 14.7 %collective-permute-start.13 = (bf16[3,64,256]{2,1,0:T(8,128)(2,1)}, bf16[3,64,256]{2,1,0:T(8,128)(2,1)S(1)}, u32[]{:S(2)}, u32[]{:S(2)}) collective-permute-start(bf16[3,64,256]{2,1,0:T(8,128)(2,1)} %get-tuple-element.161), channel_id=1, source_target_pairs={{0,2},{1,3},{2,0},{3,1},{16,18},{17,19},{18,16},{19,17},{4,6},{5,7... | collective-permute-start | bytes 294920 | tf_op jit(solution)/shard_map/ppermute | solution.py:655
  68.9 11.8 %collective-permute-start.14 = (bf16[3,64,256]{2,1,0:T(8,128)(2,1)}, bf16[3,64,256]{2,1,0:T(8,128)(2,1)S(1)}, u32[]{:S(2)}, u32[]{:S(2)}) collective-permute-start(bf16[3,64,256]{2,1,0:T(8,128)(2,1)} %get-tuple-element.162.refs_6_), channel_id=1, source_target_pairs={{0,3},{1,2},{2,1},{3,0},{16,19},{17,18},{18,17},{19,16},{4,7},{5,6... | collective-permute-start | bytes 294920 | tf_op jit(solution)/shard_map/ppermute | solution.py:655
  91.5 17.5 %collective-permute-start.19 = (bf16[4,192,128]{2,1,0:T(8,128)(2,1)}, bf16[4,192,128]{2,1,0:T(8,128)(2,1)S(1)}, u32[]{:S(2)}, u32[]{:S(2)}) collective-permute-start(bf16[4,192,128]{2,1,0:T(8,128)(2,1)} %get-tuple-element.166.refs_7_.refs_1_), channel_id=1, source_target_pairs={{0,4},{4,0},{8,12},{12,8},{16,20},{20,16},{24,28},{28,24},{1,5},{5... | collective-permute-start | bytes 589832 | tf_op jit(solution)/shard_map/ppermute | solution.py:655
  93.0 16.3 %collective-permute-start.20 = (bf16[4,192,128]{2,1,0:T(8,128)(2,1)}, bf16[4,192,128]{2,1,0:T(8,128)(2,1)S(1)}, u32[]{:S(2)}, u32[]{:S(2)}) collective-permute-start(bf16[4,192,128]{2,1,0:T(8,128)(2,1)} %get-tuple-element.166.refs_7_.refs_1_), channel_id=1, source_target_pairs={{0,8},{4,12},{8,0},{12,4},{16,24},{20,28},{24,16},{28,20},{1,9},{5... | collective-permute-start | bytes 589832 | tf_op jit(solution)/shard_map/ppermute | solution.py:655
  99.8 18.9 %collective-permute-start.16 = (bf16[1024,128]{1,0:T(8,128)(2,1)}, bf16[1024,128]{1,0:T(8,128)(2,1)S(1)}, u32[]{:S(2)}, u32[]{:S(2)}) collective-permute-start(bf16[1024,128]{1,0:T(8,128)(2,1)} %get-tuple-element.167.refs_1_), channel_id=1, source_target_pairs={{0,4},{4,0},{8,12},{12,8},{1,5},{5,1},{9,13},{13,9},{2,6},{6,2},{1... | collective-permute-start | bytes 786440 | tf_op jit(solution)/shard_map/ppermute | solution.py:655
  101.7 17.0 %collective-permute-start.17 = (bf16[1024,128]{1,0:T(8,128)(2,1)}, bf16[1024,128]{1,0:T(8,128)(2,1)S(1)}, u32[]{:S(2)}, u32[]{:S(2)}) collective-permute-start(bf16[1024,128]{1,0:T(8,128)(2,1)} %get-tuple-element.167.refs_1_), channel_id=1, source_target_pairs={{0,8},{4,12},{8,0},{12,4},{1,9},{5,13},{9,1},{13,5},{2,10},{6,14},... | collective-permute-start | bytes 786440 | tf_op jit(solution)/shard_map/ppermute | solution.py:655
  104.3 14.4 %collective-permute-start.18 = (bf16[1024,128]{1,0:T(8,128)(2,1)}, bf16[1024,128]{1,0:T(8,128)(2,1)S(1)}, u32[]{:S(2)}, u32[]{:S(2)}) collective-permute-start(bf16[1024,128]{1,0:T(8,128)(2,1)} %get-tuple-element.167.refs_1_), channel_id=1, source_target_pairs={{0,12},{4,8},{8,4},{12,0},{1,13},{5,9},{9,5},{13,1},{2,14},{6,10},... | collective-permute-start | bytes 786440 | tf_op jit(solution)/shard_map/ppermute | solution.py:655
  109.3 18.9 %collective-permute-start.26 = (bf16[1024,128]{1,0:T(8,128)(2,1)}, bf16[1024,128]{1,0:T(8,128)(2,1)S(1)}, u32[]{:S(2)}, u32[]{:S(2)}) collective-permute-start(bf16[1024,128]{1,0:T(8,128)(2,1)} %get-tuple-element.169.refs_5_.refs_7_.refs_9_.refs_11_), channel_id=1, source_target_pairs={{0,16},{4,20},{8,24},{12,28},{16,0},{20,4},{24,8},{28,12},{1,17},{... | collective-permute-start | bytes 786440 | tf_op jit(solution)/shard_map/ppermute | solution.py:662
  138.2 21.2 %collective-permute-start.33 = (bf16[1024,128]{1,0:T(8,128)(2,1)}, bf16[1024,128]{1,0:T(8,128)(2,1)S(1)}, u32[]{:S(2)}, u32[]{:S(2)}) collective-permute-start(bf16[1024,128]{1,0:T(8,128)(2,1)} %get-tuple-element.173.refs_2_), channel_id=1, source_target_pairs={{0,4},{4,0},{8,12},{12,8},{1,5},{5,1},{9,13},{13,9},{2,6},{6,2},{1... | collective-permute-start | bytes 786440 | tf_op jit(solution)/shard_map/ppermute | solution.py:655
  140.8 12.9 %collective-permute-start.36 = (bf16[3,256,128]{2,1,0:T(8,128)(2,1)S(1)}, bf16[3,256,128]{2,1,0:T(8,128)(2,1)S(1)}, u32[]{:S(2)}, u32[]{:S(2)}) collective-permute-start(bf16[3,256,128]{2,1,0:T(8,128)(2,1)S(1)} %copy-done.112), channel_id=1, source_target_pairs={{0,4},{4,0},{8,12},{12,8},{16,20},{20,16},{24,28},{28,24},{1,5},{5... | collective-permute-start | bytes 589832 | tf_op jit(solution)/shard_map/ppermute | solution.py:655
  142.3 14.1 %collective-permute-start.37 = (bf16[3,256,128]{2,1,0:T(8,128)(2,1)S(1)}, bf16[3,256,128]{2,1,0:T(8,128)(2,1)S(1)}, u32[]{:S(2)}, u32[]{:S(2)}) collective-permute-start(bf16[3,256,128]{2,1,0:T(8,128)(2,1)S(1)} %copy-done.111), channel_id=1, source_target_pairs={{0,8},{4,12},{8,0},{12,4},{16,24},{20,28},{24,16},{28,20},{1,9},{5... | collective-permute-start | bytes 589832 | tf_op jit(solution)/shard_map/ppermute | solution.py:655
  144.1 15.0 %collective-permute-start.38 = (bf16[3,256,128]{2,1,0:T(8,128)(2,1)S(1)}, bf16[3,256,128]{2,1,0:T(8,128)(2,1)S(1)}, u32[]{:S(2)}, u32[]{:S(2)}) collective-permute-start(bf16[3,256,128]{2,1,0:T(8,128)(2,1)S(1)} %copy-done.50), channel_id=1, source_target_pairs={{0,12},{4,8},{8,4},{12,0},{16,28},{20,24},{24,20},{28,16},{1,13},{... | collective-permute-start | bytes 589832 | tf_op jit(solution)/shard_map/ppermute | solution.py:655
  144.5 21.6 %collective-permute-start.34 = (bf16[1024,128]{1,0:T(8,128)(2,1)}, bf16[1024,128]{1,0:T(8,128)(2,1)S(1)}, u32[]{:S(2)}, u32[]{:S(2)}) collective-permute-start(bf16[1024,128]{1,0:T(8,128)(2,1)} %get-tuple-element.173.refs_2_), channel_id=1, source_target_pairs={{0,8},{4,12},{8,0},{12,4},{1,9},{5,13},{9,1},{13,5},{2,10},{6,14},... | collective-permute-start | bytes 786440 | tf_op jit(solution)/shard_map/ppermute | solution.py:655
  153.7 12.4 %collective-permute-start.35 = (bf16[1024,128]{1,0:T(8,128)(2,1)S(1)}, bf16[1024,128]{1,0:T(8,128)(2,1)S(1)}, u32[]{:S(2)}, u32[]{:S(2)}) collective-permute-start(bf16[1024,128]{1,0:T(8,128)(2,1)S(1)} %copy-done.8), channel_id=1, source_target_pairs={{0,12},{4,8},{8,4},{12,0},{1,13},{5,9},{9,5},{13,1},{2,14},{6,10},... | collective-permute-start | bytes 786440 | tf_op jit(solution)/shard_map/ppermute | solution.py:655
  156.3 25.9 %collective-permute-start.30 = (bf16[1024,128]{1,0:T(8,128)(2,1)}, bf16[1024,128]{1,0:T(8,128)(2,1)S(1)}, u32[]{:S(2)}, u32[]{:S(2)}) collective-permute-start(bf16[1024,128]{1,0:T(8,128)(2,1)} %get-tuple-element.172.refs_2_.refs_0_.refs_1_), channel_id=1, source_target_pairs={{0,4},{4,0},{8,12},{12,8},{16,20},{20,16},{24,28},{28,24},{1,5},{5... | collective-permute-start | bytes 786440 | tf_op jit(solution)/shard_map/ppermute | solution.py:655
  159.1 23.8 %collective-permute-start.31 = (bf16[1024,128]{1,0:T(8,128)(2,1)}, bf16[1024,128]{1,0:T(8,128)(2,1)S(1)}, u32[]{:S(2)}, u32[]{:S(2)}) collective-permute-start(bf16[1024,128]{1,0:T(8,128)(2,1)} %get-tuple-element.172.refs_2_.refs_0_.refs_1_), channel_id=1, source_target_pairs={{0,8},{4,12},{8,0},{12,4},{16,24},{20,28},{24,16},{28,20},{1,9},{5... | collective-permute-start | bytes 786440 | tf_op jit(solution)/shard_map/ppermute | solution.py:655
  159.5 32.4 %collective-permute-start.32 = (bf16[1024,128]{1,0:T(8,128)(2,1)}, bf16[1024,128]{1,0:T(8,128)(2,1)S(1)}, u32[]{:S(2)}, u32[]{:S(2)}) collective-permute-start(bf16[1024,128]{1,0:T(8,128)(2,1)} %get-tuple-element.172.refs_2_.refs_0_.refs_1_), channel_id=1, source_target_pairs={{0,12},{4,8},{8,4},{12,0},{16,28},{20,24},{24,20},{28,16},{1,13},{... | collective-permute-start | bytes 786440 | tf_op jit(solution)/shard_map/ppermute | solution.py:655
  180.8 30.5 %collective-permute-start.43 = (bf16[2,256,512]{2,1,0:T(8,128)(2,1)}, bf16[2,256,512]{2,1,0:T(8,128)(2,1)S(1)}, u32[]{:S(2)}, u32[]{:S(2)}) collective-permute-start(bf16[2,256,512]{2,1,0:T(8,128)(2,1)} %get-tuple-element.179), channel_id=1, source_target_pairs={{16,20},{20,16},{24,28},{28,24},{17,21},{21,17},{25,29},{29,25},{1... | collective-permute-start | bytes 1572872 | tf_op jit(solution)/shard_map/ppermute | solution.py:655
  181.5 29.8 %collective-permute-start.44 = (bf16[2,256,512]{2,1,0:T(8,128)(2,1)}, bf16[2,256,512]{2,1,0:T(8,128)(2,1)S(1)}, u32[]{:S(2)}, u32[]{:S(2)}) collective-permute-start(bf16[2,256,512]{2,1,0:T(8,128)(2,1)} %get-tuple-element.180), channel_id=1, source_target_pairs={{16,24},{20,28},{24,16},{28,20},{17,25},{21,29},{25,17},{29,21},{1... | collective-permute-start | bytes 1572872 | tf_op jit(solution)/shard_map/ppermute | solution.py:655
  182.2 29.1 %collective-permute-start.45 = (bf16[2,256,512]{2,1,0:T(8,128)(2,1)}, bf16[2,256,512]{2,1,0:T(8,128)(2,1)S(1)}, u32[]{:S(2)}, u32[]{:S(2)}) collective-permute-start(bf16[2,256,512]{2,1,0:T(8,128)(2,1)} %get-tuple-element.181.refs_4_), channel_id=1, source_target_pairs={{16,28},{20,24},{24,20},{28,16},{17,29},{21,25},{25,21},{29,17},{1... | collective-permute-start | bytes 1572872 | tf_op jit(solution)/shard_map/ppermute | solution.py:655
  182.9 10.2 %collective-permute-start.39 = (bf16[3,256,128]{2,1,0:T(8,128)(2,1)}, bf16[3,256,128]{2,1,0:T(8,128)(2,1)S(1)}, u32[]{:S(2)}, u32[]{:S(2)}) collective-permute-start(bf16[3,256,128]{2,1,0:T(8,128)(2,1)} %get-tuple-element.177), channel_id=1, source_target_pairs={{0,16},{4,20},{8,24},{12,28},{16,0},{20,4},{24,8},{28,12},{1,17},{... | collective-permute-start | bytes 589832 | tf_op jit(solution)/shard_map/ppermute | solution.py:662
  191.8 11.7 %collective-permute-start.40 = (bf16[3,256,128]{2,1,0:T(8,128)(2,1)}, bf16[3,256,128]{2,1,0:T(8,128)(2,1)S(1)}, u32[]{:S(2)}, u32[]{:S(2)}) collective-permute-start(bf16[3,256,128]{2,1,0:T(8,128)(2,1)} %get-tuple-element.177), channel_id=1, source_target_pairs={{0,20},{4,16},{8,28},{12,24},{16,4},{20,0},{24,12},{28,8},{1,21},{... | collective-permute-start | bytes 589832 | tf_op jit(solution)/shard_map/ppermute | solution.py:662
  193.1 12.9 %collective-permute-start.41 = (bf16[3,256,128]{2,1,0:T(8,128)(2,1)}, bf16[3,256,128]{2,1,0:T(8,128)(2,1)S(1)}, u32[]{:S(2)}, u32[]{:S(2)}) collective-permute-start(bf16[3,256,128]{2,1,0:T(8,128)(2,1)} %get-tuple-element.177), channel_id=1, source_target_pairs={{0,24},{4,28},{8,16},{12,20},{16,8},{20,12},{24,0},{28,4},{1,25},{... | collective-permute-start | bytes 589832 | tf_op jit(solution)/shard_map/ppermute | solution.py:662
  253.0 10.1 %collective-permute-start.54 = (bf16[1024,128]{1,0:T(8,128)(2,1)}, bf16[1024,128]{1,0:T(8,128)(2,1)S(1)}, u32[]{:S(2)}, u32[]{:S(2)}) collective-permute-start(bf16[1024,128]{1,0:T(8,128)(2,1)} %get-tuple-element.207), channel_id=1, source_target_pairs={{16,20},{20,16},{24,28},{28,24},{17,21},{21,17},{25,29},{29,25},{1... | collective-permute-start | bytes 786440 | tf_op jit(solution)/shard_map/ppermute | solution.py:655
  253.7 10.9 %collective-permute-start.55 = (bf16[1024,128]{1,0:T(8,128)(2,1)}, bf16[1024,128]{1,0:T(8,128)(2,1)S(1)}, u32[]{:S(2)}, u32[]{:S(2)}) collective-permute-start(bf16[1024,128]{1,0:T(8,128)(2,1)} %get-tuple-element.208), channel_id=1, source_target_pairs={{16,24},{20,28},{24,16},{28,20},{17,25},{21,29},{25,17},{29,21},{1... | collective-permute-start | bytes 786440 | tf_op jit(solution)/shard_map/ppermute | solution.py:655
  254.4 12.0 %collective-permute-start.56 = (bf16[1024,128]{1,0:T(8,128)(2,1)}, bf16[1024,128]{1,0:T(8,128)(2,1)S(1)}, u32[]{:S(2)}, u32[]{:S(2)}) collective-permute-start(bf16[1024,128]{1,0:T(8,128)(2,1)} %get-tuple-element.191.refs_15_), channel_id=1, source_target_pairs={{16,28},{20,24},{24,20},{28,16},{17,29},{21,25},{25,21},{29,17},{1... | collective-permute-start | bytes 786440 | tf_op jit(solution)/shard_map/ppermute | solution.py:655
  255.1 15.3 %collective-permute-start.53 = (bf16[3,64,128]{2,1,0:T(8,128)(2,1)S(1)}, bf16[3,64,128]{2,1,0:T(8,128)(2,1)S(1)}, u32[]{:S(2)}, u32[]{:S(2)}) collective-permute-start(bf16[3,64,128]{2,1,0:T(8,128)(2,1)S(1)} %copy-done.89), channel_id=1, source_target_pairs={{0,28},{4,24},{8,20},{12,16},{16,12},{20,8},{24,4},{28,0},{1,29},{... | collective-permute-start | bytes 147464 | tf_op jit(solution)/shard_map/ppermute | solution.py:662
  286.2 151.3 %reduce-scatter.3.cloned.1.call-start = ((), (), s32[]{:S(2)}) async-start(), calls=%async_computation.2 | async-start | bytes 2949120 | tf_op jit(solution)/shard_map/reduce_scatter | solution.py:1628
  287.1 11.1 %collective-permute-start.57 = (bf16[2,256,512]{2,1,0:T(8,128)(2,1)S(1)}, bf16[2,256,512]{2,1,0:T(8,128)(2,1)S(1)}, u32[]{:S(2)}, u32[]{:S(2)}) collective-permute-start(bf16[2,256,512]{2,1,0:T(8,128)(2,1)S(1)} %copy-done.103), channel_id=1, source_target_pairs={{0,4},{4,0},{8,12},{12,8},{1,5},{5,1},{9,13},{13,9},{2,6},{6,2},{1... | collective-permute-start | bytes 1572872 | tf_op jit(solution)/shard_map/ppermute | solution.py:655
  290.1 16.7 %collective-permute-start.58 = (bf16[2,256,512]{2,1,0:T(8,128)(2,1)S(1)}, bf16[2,256,512]{2,1,0:T(8,128)(2,1)S(1)}, u32[]{:S(2)}, u32[]{:S(2)}) collective-permute-start(bf16[2,256,512]{2,1,0:T(8,128)(2,1)S(1)} %copy-done.102), channel_id=1, source_target_pairs={{0,8},{4,12},{8,0},{12,4},{1,9},{5,13},{9,1},{13,5},{2,10},{6,14},... | collective-permute-start | bytes 1572872 | tf_op jit(solution)/shard_map/ppermute | solution.py:655
  292.7 14.1 %collective-permute-start.59 = (bf16[2,256,512]{2,1,0:T(8,128)(2,1)S(1)}, bf16[2,256,512]{2,1,0:T(8,128)(2,1)S(1)}, u32[]{:S(2)}, u32[]{:S(2)}) collective-permute-start(bf16[2,256,512]{2,1,0:T(8,128)(2,1)S(1)} %copy-done.101), channel_id=1, source_target_pairs={{0,12},{4,8},{8,4},{12,0},{1,13},{5,9},{9,5},{13,1},{2,14},{6,10},... | collective-permute-start | bytes 1572872 | tf_op jit(solution)/shard_map/ppermute | solution.py:655
  296.4 22.6 %collective-permute-start.69 = (bf16[256,128]{1,0:T(8,128)(2,1)S(1)}, bf16[256,128]{1,0:T(8,128)(2,1)S(1)}, u32[]{:S(2)}, u32[]{:S(2)}) collective-permute-start(bf16[256,128]{1,0:T(8,128)(2,1)S(1)} %copy-done.125), channel_id=1, source_target_pairs={{0,16},{4,20},{8,24},{12,28},{16,0},{20,4},{24,8},{28,12},{1,17},{... | collective-permute-start | bytes 196616 | tf_op jit(solution)/shard_map/ppermute | solution.py:662
  296.5 24.1 %collective-permute-start.70 = (bf16[256,128]{1,0:T(8,128)(2,1)S(1)}, bf16[256,128]{1,0:T(8,128)(2,1)S(1)}, u32[]{:S(2)}, u32[]{:S(2)}) collective-permute-start(bf16[256,128]{1,0:T(8,128)(2,1)S(1)} %copy-done.124), channel_id=1, source_target_pairs={{0,20},{4,16},{8,28},{12,24},{16,4},{20,0},{24,12},{28,8},{1,21},{... | collective-permute-start | bytes 196616 | tf_op jit(solution)/shard_map/ppermute | solution.py:662
  298.2 17.7 %collective-permute-start.49 = (f32[8,128]{1,0:T(8,128)S(1)}, f32[8,128]{1,0:T(8,128)S(1)}, u32[]{:S(2)}, u32[]{:S(2)}) collective-permute-start(f32[8,128]{1,0:T(8,128)S(1)} %copy-done.97), channel_id=1, source_target_pairs={{0,16},{4,20},{8,24},{12,28},{16,0},{20,4},{24,8},{28,12},{1,17},{... | collective-permute-start | bytes 12296 | tf_op jit(solution)/shard_map/ppermute | solution.py:662
  306.8 18.5 %collective-permute-start.71 = (bf16[256,128]{1,0:T(8,128)(2,1)S(1)}, bf16[256,128]{1,0:T(8,128)(2,1)S(1)}, u32[]{:S(2)}, u32[]{:S(2)}) collective-permute-start(bf16[256,128]{1,0:T(8,128)(2,1)S(1)} %copy-done.123), channel_id=1, source_target_pairs={{0,24},{4,28},{8,16},{12,20},{16,8},{20,12},{24,0},{28,4},{1,25},{... | collective-permute-start | bytes 196616 | tf_op jit(solution)/shard_map/ppermute | solution.py:662
  306.8 18.5 %collective-permute-start.72 = (bf16[256,128]{1,0:T(8,128)(2,1)S(1)}, bf16[256,128]{1,0:T(8,128)(2,1)S(1)}, u32[]{:S(2)}, u32[]{:S(2)}) collective-permute-start(bf16[256,128]{1,0:T(8,128)(2,1)S(1)} %copy-done.122), channel_id=1, source_target_pairs={{0,28},{4,24},{8,20},{12,16},{16,12},{20,8},{24,4},{28,0},{1,29},{... | collective-permute-start | bytes 196616 | tf_op jit(solution)/shard_map/ppermute | solution.py:662
  362.3 11.1 %collective-permute-start.65 = (bf16[6,128,128]{2,1,0:T(8,128)(2,1)S(1)}, bf16[6,128,128]{2,1,0:T(8,128)(2,1)S(1)}, u32[]{:S(2)}, u32[]{:S(2)}) collective-permute-start(bf16[6,128,128]{2,1,0:T(8,128)(2,1)S(1)} %copy-done.54), channel_id=1, source_target_pairs={{0,12},{4,8},{8,4},{12,0},{16,28},{20,24},{24,20},{28,16},{1,13},{... | collective-permute-start | bytes 589832 | tf_op jit(solution)/shard_map/ppermute | solution.py:655
  366.1 17.0 %collective-permute-start.62 = (bf16[3,256,128]{2,1,0:T(8,128)(2,1)S(1)}, bf16[3,256,128]{2,1,0:T(8,128)(2,1)S(1)}, u32[]{:S(2)}, u32[]{:S(2)}) collective-permute-start(bf16[3,256,128]{2,1,0:T(8,128)(2,1)S(1)} %copy-done.49), channel_id=1, source_target_pairs={{0,12},{4,8},{8,4},{12,0},{16,28},{20,24},{24,20},{28,16},{1,13},{... | collective-permute-start | bytes 589832 | tf_op jit(solution)/shard_map/ppermute | solution.py:655
  369.8 10.3 %collective-permute-start.61 = (bf16[3,256,128]{2,1,0:T(8,128)(2,1)S(1)}, bf16[3,256,128]{2,1,0:T(8,128)(2,1)S(1)}, u32[]{:S(2)}, u32[]{:S(2)}) collective-permute-start(bf16[3,256,128]{2,1,0:T(8,128)(2,1)S(1)} %copy-done.110), channel_id=1, source_target_pairs={{0,8},{4,12},{8,0},{12,4},{16,24},{20,28},{24,16},{28,20},{1,9},{5... | collective-permute-start | bytes 589832 | tf_op jit(solution)/shard_map/ppermute | solution.py:655
  372.2 24.8 %collective-permute-start.81 = (bf16[256,512]{1,0:T(8,128)(2,1)S(1)}, bf16[256,512]{1,0:T(8,128)(2,1)S(1)}, u32[]{:S(2)}, u32[]{:S(2)}) collective-permute-start(bf16[256,512]{1,0:T(8,128)(2,1)S(1)} %copy-done.27), channel_id=1, source_target_pairs={{0,12},{4,8},{8,4},{12,0},{16,28},{20,24},{24,20},{28,16},{1,13},{... | collective-permute-start | bytes 786440 | tf_op jit(solution)/shard_map/ppermute | solution.py:655
  373.4 19.7 %collective-permute-start.79 = (bf16[256,512]{1,0:T(8,128)(2,1)S(1)}, bf16[256,512]{1,0:T(8,128)(2,1)S(1)}, u32[]{:S(2)}, u32[]{:S(2)}) collective-permute-start(bf16[256,512]{1,0:T(8,128)(2,1)S(1)} %copy-done.105), channel_id=1, source_target_pairs={{0,4},{4,0},{8,12},{12,8},{16,20},{20,16},{24,28},{28,24},{1,5},{5... | collective-permute-start | bytes 786440 | tf_op jit(solution)/shard_map/ppermute | solution.py:655
  374.0 23.0 %collective-permute-start.80 = (bf16[256,512]{1,0:T(8,128)(2,1)S(1)}, bf16[256,512]{1,0:T(8,128)(2,1)S(1)}, u32[]{:S(2)}, u32[]{:S(2)}) collective-permute-start(bf16[256,512]{1,0:T(8,128)(2,1)S(1)} %copy-done.104), channel_id=1, source_target_pairs={{0,8},{4,12},{8,0},{12,4},{16,24},{20,28},{24,16},{28,20},{1,9},{5... | collective-permute-start | bytes 786440 | tf_op jit(solution)/shard_map/ppermute | solution.py:655
  392.4 40.7 %collective-permute-start.76 = (bf16[3,64,512]{2,1,0:T(8,128)(2,1)}, bf16[3,64,512]{2,1,0:T(8,128)(2,1)S(1)}, u32[]{:S(2)}, u32[]{:S(2)}) collective-permute-start(bf16[3,64,512]{2,1,0:T(8,128)(2,1)} %get-tuple-element.260), channel_id=1, source_target_pairs={{0,1},{1,0},{2,3},{3,2},{16,17},{17,16},{18,19},{19,18},{4,5},{5,4... | collective-permute-start | bytes 589832 | tf_op jit(solution)/shard_map/ppermute | solution.py:655
  392.5 42.8 %collective-permute-start.77 = (bf16[3,64,512]{2,1,0:T(8,128)(2,1)}, bf16[3,64,512]{2,1,0:T(8,128)(2,1)S(1)}, u32[]{:S(2)}, u32[]{:S(2)}) collective-permute-start(bf16[3,64,512]{2,1,0:T(8,128)(2,1)} %get-tuple-element.261), channel_id=1, source_target_pairs={{0,2},{1,3},{2,0},{3,1},{16,18},{17,19},{18,16},{19,17},{4,6},{5,7... | collective-permute-start | bytes 589832 | tf_op jit(solution)/shard_map/ppermute | solution.py:655
  393.1 42.1 %collective-permute-start.78 = (bf16[3,64,512]{2,1,0:T(8,128)(2,1)}, bf16[3,64,512]{2,1,0:T(8,128)(2,1)S(1)}, u32[]{:S(2)}, u32[]{:S(2)}) collective-permute-start(bf16[3,64,512]{2,1,0:T(8,128)(2,1)} %get-tuple-element.262.refs_5_), channel_id=1, source_target_pairs={{0,3},{1,2},{2,1},{3,0},{16,19},{17,18},{18,17},{19,16},{4,7},{5,6... | collective-permute-start | bytes 589832 | tf_op jit(solution)/shard_map/ppermute | solution.py:655
  397.0 19.5 %collective-permute-start.85 = (bf16[6,32,128]{2,1,0:T(8,128)(2,1)}, bf16[6,32,128]{2,1,0:T(8,128)(2,1)S(1)}, u32[]{:S(2)}, u32[]{:S(2)}) collective-permute-start(bf16[6,32,128]{2,1,0:T(8,128)(2,1)} %get-tuple-element.273), channel_id=1, source_target_pairs={{0,1},{1,0},{2,3},{3,2},{16,17},{17,16},{18,19},{19,18},{4,5},{5,4... | collective-permute-start | bytes 147464 | tf_op jit(solution)/shard_map/ppermute | solution.py:655
  402.1 47.2 %collective-permute-start.91 = (bf16[3,288,128]{2,1,0:T(8,128)(2,1)}, bf16[3,288,128]{2,1,0:T(8,128)(2,1)S(1)}, u32[]{:S(2)}, u32[]{:S(2)}) collective-permute-start(bf16[3,288,128]{2,1,0:T(8,128)(2,1)} %get-tuple-element.279), channel_id=1, source_target_pairs={{0,4},{4,0},{8,12},{12,8},{16,20},{20,16},{24,28},{28,24},{1,5},{5... | collective-permute-start | bytes 663560 | tf_op jit(solution)/shard_map/ppermute | solution.py:655
  416.5 14.9 %collective-permute-start.86 = (bf16[6,32,128]{2,1,0:T(8,128)(2,1)S(1)}, bf16[6,32,128]{2,1,0:T(8,128)(2,1)S(1)}, u32[]{:S(2)}, u32[]{:S(2)}) collective-permute-start(bf16[6,32,128]{2,1,0:T(8,128)(2,1)S(1)} %copy-done.133), channel_id=1, source_target_pairs={{0,2},{1,3},{2,0},{3,1},{16,18},{17,19},{18,16},{19,17},{4,6},{5,7... | collective-permute-start | bytes 147464 | tf_op jit(solution)/shard_map/ppermute | solution.py:655
  431.4 10.3 %collective-permute-start.87 = (bf16[6,32,128]{2,1,0:T(8,128)(2,1)S(1)}, bf16[6,32,128]{2,1,0:T(8,128)(2,1)S(1)}, u32[]{:S(2)}, u32[]{:S(2)}) collective-permute-start(bf16[6,32,128]{2,1,0:T(8,128)(2,1)S(1)} %copy-done.129), channel_id=1, source_target_pairs={{0,3},{1,2},{2,1},{3,0},{16,19},{17,18},{18,17},{19,16},{4,7},{5,6... | collective-permute-start | bytes 147464 | tf_op jit(solution)/shard_map/ppermute | solution.py:655
  433.1 14.6 %collective-permute-start.84 = (bf16[64,512]{1,0:T(8,128)(2,1)}, bf16[64,512]{1,0:T(8,128)(2,1)S(1)}, u32[]{:S(2)}, u32[]{:S(2)}) collective-permute-start(bf16[64,512]{1,0:T(8,128)(2,1)} %get-tuple-element.266.refs_2_), channel_id=1, source_target_pairs={{0,3},{1,2},{2,1},{3,0},{16,19},{17,18},{18,17},{19,16},{4,7},{5,6... | collective-permute-start | bytes 196616 | tf_op jit(solution)/shard_map/ppermute | solution.py:655
  435.2 10.4 %collective-permute-start.82 = (bf16[64,512]{1,0:T(8,128)(2,1)}, bf16[64,512]{1,0:T(8,128)(2,1)S(1)}, u32[]{:S(2)}, u32[]{:S(2)}) collective-permute-start(bf16[64,512]{1,0:T(8,128)(2,1)} %get-tuple-element.270), channel_id=1, source_target_pairs={{0,1},{1,0},{2,3},{3,2},{16,17},{17,16},{18,19},{19,18},{4,5},{5,4... | collective-permute-start | bytes 196616 | tf_op jit(solution)/shard_map/ppermute | solution.py:655
  435.3 11.1 %collective-permute-start.83 = (bf16[64,512]{1,0:T(8,128)(2,1)}, bf16[64,512]{1,0:T(8,128)(2,1)S(1)}, u32[]{:S(2)}, u32[]{:S(2)}) collective-permute-start(bf16[64,512]{1,0:T(8,128)(2,1)} %get-tuple-element.271), channel_id=1, source_target_pairs={{0,2},{1,3},{2,0},{3,1},{16,18},{17,19},{18,16},{19,17},{4,6},{5,7... | collective-permute-start | bytes 196616 | tf_op jit(solution)/shard_map/ppermute | solution.py:655
  441.7 12.2 %collective-permute-start.93 = (bf16[3,288,128]{2,1,0:T(8,128)(2,1)S(1)}, bf16[3,288,128]{2,1,0:T(8,128)(2,1)S(1)}, u32[]{:S(2)}, u32[]{:S(2)}) collective-permute-start(bf16[3,288,128]{2,1,0:T(8,128)(2,1)S(1)} %copy-done.106), channel_id=1, source_target_pairs={{0,12},{4,8},{8,4},{12,0},{16,28},{20,24},{24,20},{28,16},{1,13},{... | collective-permute-start | bytes 663560 | tf_op jit(solution)/shard_map/ppermute | solution.py:655
  445.6 11.8 %collective-permute-start.90 = (bf16[2,288,128]{2,1,0:T(8,128)(2,1)S(1)}, bf16[2,288,128]{2,1,0:T(8,128)(2,1)S(1)}, u32[]{:S(2)}, u32[]{:S(2)}) collective-permute-start(bf16[2,288,128]{2,1,0:T(8,128)(2,1)S(1)} %copy-done.61), channel_id=1, source_target_pairs={{0,12},{4,8},{8,4},{12,0},{16,28},{20,24},{24,20},{28,16},{1,13},{... | collective-permute-start | bytes 442376 | tf_op jit(solution)/shard_map/ppermute | solution.py:655
  447.8 9.6 %collective-permute-start.88 = (bf16[2,288,128]{2,1,0:T(8,128)(2,1)S(1)}, bf16[2,288,128]{2,1,0:T(8,128)(2,1)S(1)}, u32[]{:S(2)}, u32[]{:S(2)}) collective-permute-start(bf16[2,288,128]{2,1,0:T(8,128)(2,1)S(1)} %copy-done.118), channel_id=1, source_target_pairs={{0,4},{4,0},{8,12},{12,8},{16,20},{20,16},{24,28},{28,24},{1,5},{5... | collective-permute-start | bytes 442376 | tf_op jit(solution)/shard_map/ppermute | solution.py:655
  (174 other events, 1444.9 us)
Sparse Core Ops, SparseCore 0:
  24.1 63.3 all-gather.7
  89.7 68.6 all-gather.9
  286.3 70.5 reduce-scatter.4
  361.7 65.1 reduce-scatter.2
